TPU v7x, 32 devices: a whole 2x2x4 slice. The times are simulated.
32 devices in a mesh: dp: 2 (over x), ctx: 16 (over z, y, core).
Axes of the slice: x: 2, y: 2, z: 4, core: 2. Of those that a mesh axis runs over, the one named last changes fastest.
Arguments:
- gate_branch: bfloat16 [4096, 4096], P(('dp', 'ctx')), may hold values from -6 to 6
- conv_input: bfloat16 [4096, 4096], P(('dp', 'ctx')), may hold values from -6 to 6
- grad_output: bfloat16 [4096, 4096], P(('dp', 'ctx')), may hold values from -6 to 6
- filter_taps: float32 [256, 128], replicated, may hold values from -0.5 to 0.5
- document_lengths: int32 [2, 16], P('dp'), may hold values from 1 to 512, 2048 in all within a row
Outputs:
- grad_input: bfloat16 [4096, 4096], P(('dp', 'ctx'))
- filter_grad: float32 [256, 128], P('ctx')
Inputs may be any that keep to these rules, and one draw needn't show every extreme that they name: `document_lengths`: each row holds the lengths of 16 documents packed end to end in one data group's 2048 tokens; they sum to 2048.
All inputs are finite; a program needn't handle non-finite values.
Results may differ from a plain program's by a relative error of at most 0.0057.
Values may be sent and summed in bfloat16 or wider, within the bound.
No kernel may reach another device: no remote copies, remote signals or barrier semaphores. Data moves between devices by JAX's collectives and lax.ppermute only.
A program may use at most 128 MiB of HBM per device.

v0:
```python
import math

import jax
import jax.numpy as jnp
from jax import lax
from jax.sharding import PartitionSpec as P

GROUP = 16


def band_matrix(taps_half):
    tile_count = taps_half.shape[0]
    padded = jnp.concatenate([taps_half, jnp.zeros((tile_count, 129), taps_half.dtype)], axis=1)
    repeated = jnp.broadcast_to(padded[:, None, :], (tile_count, 128, 257)).reshape(
        tile_count, 128 * 257
    )
    return repeated[:, : 128 * 256].reshape(tile_count, 128, 256)


def lag_sums(product):
    tile_count = product.shape[0]
    flattened = product.reshape(tile_count, 128 * 256)
    flattened = jnp.concatenate([flattened, jnp.zeros((tile_count, 128), product.dtype)], axis=1)
    skewed = flattened.reshape(tile_count, 128, 257)
    column = jnp.sum(skewed, axis=1)
    return column[:, 1:129][:, ::-1]


def segment_ids(places, document_ends):
    return jnp.sum((places[..., None] >= document_ends).astype(jnp.int32), axis=-1)


def block_grads(
    mixed_here,
    mixed_after,
    input_before,
    input_here,
    labels_before,
    labels_here,
    labels_after,
    taps_half,
):
    blocks = mixed_here.shape[0]
    channels = mixed_here.shape[2]
    groups = channels // GROUP
    group_tile = min(groups, 32)
    block_tile = math.gcd(blocks, max(1, 32 // group_tile))
    group_steps = groups // group_tile
    block_steps = blocks // block_tile
    band = band_matrix(taps_half).reshape(group_steps, group_tile, 128, 256)
    mixed_ext = jnp.concatenate([mixed_here, mixed_after], axis=1)
    input_ext = jnp.concatenate([input_before, input_here], axis=1)
    keep_down = (
        labels_here[:, :, None] == jnp.concatenate([labels_here, labels_after], axis=1)[:, None, :]
    )
    keep_lag = (
        labels_here[:, :, None] == jnp.concatenate([labels_before, labels_here], axis=1)[:, None, :]
    )
    keep_down = keep_down.reshape(block_steps, block_tile, 128, 256)
    keep_lag = keep_lag.reshape(block_steps, block_tile, 128, 256)

    def to_tiles(array_in):
        return jnp.moveaxis(
            array_in.reshape(block_steps, block_tile, 256, group_steps, group_tile, GROUP), 3, 0
        )

    mixed_tiles = to_tiles(mixed_ext)
    input_tiles = to_tiles(input_ext)

    def per_group(operands):
        band_tile, mixed_part, input_part = operands

        def per_block(pieces):
            mask_down, mask_lag, mixed_block, input_block = pieces
            kernel = band_tile[None] * mask_down[:, None].astype(jnp.bfloat16)
            down_part = jnp.einsum(
                "bgij,bjgc->bigc", kernel, mixed_block, preferred_element_type=jnp.float32
            )
            product = jnp.einsum(
                "bigc,bjgc->bgij",
                mixed_block[:, :128],
                input_block,
                preferred_element_type=jnp.float32,
            )
            product = jnp.sum(jnp.where(mask_lag[:, None], product, jnp.float32(0.0)), axis=0)
            return (down_part, lag_sums(product))

        return lax.map(per_block, (keep_down, keep_lag, mixed_part, input_part))

    down_all, lagged = lax.map(per_group, (band, mixed_tiles, input_tiles))
    down_all = jnp.moveaxis(down_all, 0, 3).reshape(blocks, 128, channels).astype(jnp.bfloat16)
    lagged = jnp.sum(lagged, axis=1).reshape(groups, 128)
    return (down_all, lagged)


def shards(gate_branch, conv_input, grad_output, filter_taps, document_lengths):
    local_rows = gate_branch.shape[0]
    channels = gate_branch.shape[1]
    ctx_count = lax.axis_size("ctx")
    grad_scale = (1.0 * GROUP * lax.axis_size("dp") * local_rows * ctx_count) ** (-0.5)
    taps_half = filter_taps.astype(jnp.bfloat16)
    document_ends = jnp.cumsum(document_lengths[0])
    mixed_grad = (grad_output.astype(jnp.float32) * gate_branch.astype(jnp.float32)).astype(
        jnp.bfloat16
    )
    mixed_all, input_all = (
        lax.all_to_all(mixed_grad, "ctx", split_axis=1, concat_axis=0, tiled=True),
        lax.all_to_all(conv_input, "ctx", split_axis=1, concat_axis=0, tiled=True),
    )
    total_rows = mixed_all.shape[0]
    panel_width = channels // ctx_count
    own_groups = panel_width // GROUP
    blocks = total_rows // 128
    own_taps = lax.dynamic_slice_in_dim(
        taps_half, lax.axis_index("ctx") * own_groups, own_groups, 0
    )
    mixed_here = mixed_all.reshape(blocks, 128, panel_width)
    input_here = input_all.reshape(blocks, 128, panel_width)
    zero_block = jnp.zeros((1, 128, panel_width), jnp.bfloat16)
    mixed_after = jnp.concatenate([mixed_here[1:], zero_block], axis=0)
    input_before = jnp.concatenate([zero_block, input_here[:-1]], axis=0)
    places = jnp.arange(total_rows, dtype=jnp.int32).reshape(blocks, 128)
    labels_here = segment_ids(places, document_ends)
    labels_before = segment_ids(places - 128, document_ends)
    labels_after = segment_ids(places + 128, document_ends)
    down_all, lagged = block_grads(
        mixed_here,
        mixed_after,
        input_before,
        input_here,
        labels_before,
        labels_here,
        labels_after,
        own_taps,
    )
    grad_input = lax.all_to_all(
        down_all.reshape(total_rows, panel_width), "ctx", split_axis=0, concat_axis=1, tiled=True
    )
    filter_grad = lax.psum(lagged, "dp") * grad_scale
    return (grad_input, filter_grad)


def solution(mesh):
    placed = (
        P(("dp", "ctx"), None),
        P(("dp", "ctx"), None),
        P(("dp", "ctx"), None),
        P(),
        P("dp", None),
    )
    return jax.shard_map(
        shards,
        mesh=mesh,
        in_specs=placed,
        out_specs=(P(("dp", "ctx"), None), P("ctx", None)),
        check_vma=False,
    )
```

profile of v0, /device:TPU:0, one launch (start us, length us, event | category | flops | bytes accessed | tf_op | source)
XLA Modules:
  0.0 206.6 jit_solution(6985318860384526200)
XLA Ops:
  0.6 1.8 multiply_convert_fusion
  3.8 7.4 %all-to-all-start = ((bf16[128,16,256]{0,2,1:T(8,128)(2,1)}), bf16[128,16,256]{0,2,1:T(8,128)(2,1)S(1)}, u32[]{:S(2)}, u32[]{:S(2)}) async-start(bf16[128,16,256]{0,2,1:T(8,128)(2,1)} %bitcast.7), calls=%async_computation | async-start | bytes 2097152 | tf_op jit(solution)/shard_map/all_to_all | solution.py:107
  11.2 1.3 copy.32
  12.5 21.6 %all-to-all-done = bf16[128,16,256]{0,2,1:T(8,128)(2,1)S(1)} async-done(((bf16[128,16,256]{0,2,1:T(8,128)(2,1)}), bf16[128,16,256]{0,2,1:T(8,128)(2,1)S(1)}, u32[]{:S(2)}, u32[]{:S(2)}) %all-to-all-start) | async-done | bytes 1048608 | tf_op jit(solution)/shard_map/all_to_all | solution.py:107
  34.1 6.9 %all-to-all-start.1 = ((bf16[128,16,256]{0,2,1:T(8,128)(2,1)}), bf16[128,16,256]{0,2,1:T(8,128)(2,1)S(1)}, u32[]{:S(2)}, u32[]{:S(2)}) async-start(bf16[128,16,256]{0,2,1:T(8,128)(2,1)} %bitcast.12), calls=%async_computation.1 | async-start | bytes 2097152 | tf_op jit(solution)/shard_map/all_to_all | solution.py:108
  42.8 3.1 %reshape.112 = bf16[16,32896]{1,0:T(8,128)(2,1)S(1)} reshape(bf16[16,128,257]{2,1,0:T(8,128)(2,1)} %broadcast_in_dim.22) | data formatting | bytes 2105344 | tf_op jit(solution)/shard_map/reshape | solution.py:14
  47.2 1.5 broadcast_compare_fusion
  48.8 1.6 fusion.16
  50.4 13.5 %all-to-all-done.1 = bf16[128,16,256]{0,2,1:T(8,128)(2,1)S(1)} async-done(((bf16[128,16,256]{0,2,1:T(8,128)(2,1)}), bf16[128,16,256]{0,2,1:T(8,128)(2,1)S(1)}, u32[]{:S(2)}, u32[]{:S(2)}) %all-to-all-start.1) | async-done | bytes 1048608 | tf_op jit(solution)/shard_map/all_to_all | solution.py:108
  64.1 1.6 pad_maximum_fusion
  65.8 106.8 %while.21 = (s32[]{:T(128)}, bf16[8,2,128,16,16]{2,4,3,1,0:T(8,128)(2,1)}, f32[8,16,128]{2,1,0:T(8,128)S(1)}, bf16[8,2,256,16,16]{2,4,3,1,0:T(8,128)(2,1)}, bf16...) while((s32[]{:T(128)}, ...), condition=%wide.region_7.8_spmd, body=%wide.region_4.7_spmd.sunk | while | flops 70318064 | bytes 19891396 | solution.py:88
  67.6 2.6 %fusion.26 = bf16[8,2,128,16,16]{2,4,3,1,0:T(8,128)(2,1)} fusion(bf16[8,2,128,16,16]{2,4,3,1,0:T(8,128)(2,1)} %get-tuple-element.166, s32[]{:T(128)S(6)} %copy.42, bf16[2,128,256]{2,1,0:T(8,128)(2,1)S(1)} %get-tuple-element.153, bf16[16,128,256]{2,1,0:T(8,128)(2,1)} %get-tuple-element.179, bf16[8,2,256,16,16]{2,4,3,1,0:T(8,128)(2,1)} %get-tuple-element.178), kind=kOutput, calls=%fused_computation.4.clone.1 | convolution fusion | flops 34603008 | bytes 1704960 | tf_op jit(solution)/shard_map/while/body/eval_jaxpr/while/body/eval_jaxpr/bgij,bjgc->bigc/dot_general | solution.py:76
  70.3 2.0 select_reduce_fusion.2
  73.5 1.5 concatenate.39
  75.0 3.7 %reshape.118 = f32[16,128,257]{2,1,0:T(8,128)S(1)} reshape(f32[16,32896]{1,0:T(8,128)} %concatenate.39) | data formatting | bytes 4210688 | tf_op jit(solution)/shard_map/while/body/eval_jaxpr/while/body/eval_jaxpr/reshape | solution.py:24
  81.0 2.6 %fusion.26 = bf16[8,2,128,16,16]{2,4,3,1,0:T(8,128)(2,1)} fusion(bf16[8,2,128,16,16]{2,4,3,1,0:T(8,128)(2,1)} %get-tuple-element.166, s32[]{:T(128)S(6)} %copy.42, bf16[2,128,256]{2,1,0:T(8,128)(2,1)S(1)} %get-tuple-element.153, bf16[16,128,256]{2,1,0:T(8,128)(2,1)} %get-tuple-element.179, bf16[8,2,256,16,16]{2,4,3,1,0:T(8,128)(2,1)} %get-tuple-element.178), kind=kOutput, calls=%fused_computation.4.clone.1 | convolution fusion | flops 34603008 | bytes 1704960 | tf_op jit(solution)/shard_map/while/body/eval_jaxpr/while/body/eval_jaxpr/bgij,bjgc->bigc/dot_general | solution.py:76
  83.6 2.0 select_reduce_fusion.2
  86.9 1.5 concatenate.39
  88.4 3.7 %reshape.118 = f32[16,128,257]{2,1,0:T(8,128)S(1)} reshape(f32[16,32896]{1,0:T(8,128)} %concatenate.39) | data formatting | bytes 4210688 | tf_op jit(solution)/shard_map/while/body/eval_jaxpr/while/body/eval_jaxpr/reshape | solution.py:24
  94.3 2.6 %fusion.26 = bf16[8,2,128,16,16]{2,4,3,1,0:T(8,128)(2,1)} fusion(bf16[8,2,128,16,16]{2,4,3,1,0:T(8,128)(2,1)} %get-tuple-element.166, s32[]{:T(128)S(6)} %copy.42, bf16[2,128,256]{2,1,0:T(8,128)(2,1)S(1)} %get-tuple-element.153, bf16[16,128,256]{2,1,0:T(8,128)(2,1)} %get-tuple-element.179, bf16[8,2,256,16,16]{2,4,3,1,0:T(8,128)(2,1)} %get-tuple-element.178), kind=kOutput, calls=%fused_computation.4.clone.1 | convolution fusion | flops 34603008 | bytes 1704960 | tf_op jit(solution)/shard_map/while/body/eval_jaxpr/while/body/eval_jaxpr/bgij,bjgc->bigc/dot_general | solution.py:76
  97.0 2.0 select_reduce_fusion.2
  100.2 1.5 concatenate.39
  101.7 3.7 %reshape.118 = f32[16,128,257]{2,1,0:T(8,128)S(1)} reshape(f32[16,32896]{1,0:T(8,128)} %concatenate.39) | data formatting | bytes 4210688 | tf_op jit(solution)/shard_map/while/body/eval_jaxpr/while/body/eval_jaxpr/reshape | solution.py:24
  107.7 2.6 %fusion.26 = bf16[8,2,128,16,16]{2,4,3,1,0:T(8,128)(2,1)} fusion(bf16[8,2,128,16,16]{2,4,3,1,0:T(8,128)(2,1)} %get-tuple-element.166, s32[]{:T(128)S(6)} %copy.42, bf16[2,128,256]{2,1,0:T(8,128)(2,1)S(1)} %get-tuple-element.153, bf16[16,128,256]{2,1,0:T(8,128)(2,1)} %get-tuple-element.179, bf16[8,2,256,16,16]{2,4,3,1,0:T(8,128)(2,1)} %get-tuple-element.178), kind=kOutput, calls=%fused_computation.4.clone.1 | convolution fusion | flops 34603008 | bytes 1704960 | tf_op jit(solution)/shard_map/while/body/eval_jaxpr/while/body/eval_jaxpr/bgij,bjgc->bigc/dot_general | solution.py:76
  110.3 2.0 select_reduce_fusion.2
  113.6 1.5 concatenate.39
  115.1 3.7 %reshape.118 = f32[16,128,257]{2,1,0:T(8,128)S(1)} reshape(f32[16,32896]{1,0:T(8,128)} %concatenate.39) | data formatting | bytes 4210688 | tf_op jit(solution)/shard_map/while/body/eval_jaxpr/while/body/eval_jaxpr/reshape | solution.py:24
  121.0 2.6 %fusion.26 = bf16[8,2,128,16,16]{2,4,3,1,0:T(8,128)(2,1)} fusion(bf16[8,2,128,16,16]{2,4,3,1,0:T(8,128)(2,1)} %get-tuple-element.166, s32[]{:T(128)S(6)} %copy.42, bf16[2,128,256]{2,1,0:T(8,128)(2,1)S(1)} %get-tuple-element.153, bf16[16,128,256]{2,1,0:T(8,128)(2,1)} %get-tuple-element.179, bf16[8,2,256,16,16]{2,4,3,1,0:T(8,128)(2,1)} %get-tuple-element.178), kind=kOutput, calls=%fused_computation.4.clone.1 | convolution fusion | flops 34603008 | bytes 1704960 | tf_op jit(solution)/shard_map/while/body/eval_jaxpr/while/body/eval_jaxpr/bgij,bjgc->bigc/dot_general | solution.py:76
  123.7 2.0 select_reduce_fusion.2
  126.9 1.5 concatenate.39
  128.4 3.7 %reshape.118 = f32[16,128,257]{2,1,0:T(8,128)S(1)} reshape(f32[16,32896]{1,0:T(8,128)} %concatenate.39) | data formatting | bytes 4210688 | tf_op jit(solution)/shard_map/while/body/eval_jaxpr/while/body/eval_jaxpr/reshape | solution.py:24
  134.4 2.6 %fusion.26 = bf16[8,2,128,16,16]{2,4,3,1,0:T(8,128)(2,1)} fusion(bf16[8,2,128,16,16]{2,4,3,1,0:T(8,128)(2,1)} %get-tuple-element.166, s32[]{:T(128)S(6)} %copy.42, bf16[2,128,256]{2,1,0:T(8,128)(2,1)S(1)} %get-tuple-element.153, bf16[16,128,256]{2,1,0:T(8,128)(2,1)} %get-tuple-element.179, bf16[8,2,256,16,16]{2,4,3,1,0:T(8,128)(2,1)} %get-tuple-element.178), kind=kOutput, calls=%fused_computation.4.clone.1 | convolution fusion | flops 34603008 | bytes 1704960 | tf_op jit(solution)/shard_map/while/body/eval_jaxpr/while/body/eval_jaxpr/bgij,bjgc->bigc/dot_general | solution.py:76
  137.0 2.0 select_reduce_fusion.2
  140.3 1.5 concatenate.39
  141.7 3.7 %reshape.118 = f32[16,128,257]{2,1,0:T(8,128)S(1)} reshape(f32[16,32896]{1,0:T(8,128)} %concatenate.39) | data formatting | bytes 4210688 | tf_op jit(solution)/shard_map/while/body/eval_jaxpr/while/body/eval_jaxpr/reshape | solution.py:24
  147.7 2.6 %fusion.26 = bf16[8,2,128,16,16]{2,4,3,1,0:T(8,128)(2,1)} fusion(bf16[8,2,128,16,16]{2,4,3,1,0:T(8,128)(2,1)} %get-tuple-element.166, s32[]{:T(128)S(6)} %copy.42, bf16[2,128,256]{2,1,0:T(8,128)(2,1)S(1)} %get-tuple-element.153, bf16[16,128,256]{2,1,0:T(8,128)(2,1)} %get-tuple-element.179, bf16[8,2,256,16,16]{2,4,3,1,0:T(8,128)(2,1)} %get-tuple-element.178), kind=kOutput, calls=%fused_computation.4.clone.1 | convolution fusion | flops 34603008 | bytes 1704960 | tf_op jit(solution)/shard_map/while/body/eval_jaxpr/while/body/eval_jaxpr/bgij,bjgc->bigc/dot_general | solution.py:76
  150.4 2.0 select_reduce_fusion.2
  153.6 1.5 concatenate.39
  155.1 3.7 %reshape.118 = f32[16,128,257]{2,1,0:T(8,128)S(1)} reshape(f32[16,32896]{1,0:T(8,128)} %concatenate.39) | data formatting | bytes 4210688 | tf_op jit(solution)/shard_map/while/body/eval_jaxpr/while/body/eval_jaxpr/reshape | solution.py:24
  161.1 2.6 %fusion.26 = bf16[8,2,128,16,16]{2,4,3,1,0:T(8,128)(2,1)} fusion(bf16[8,2,128,16,16]{2,4,3,1,0:T(8,128)(2,1)} %get-tuple-element.166, s32[]{:T(128)S(6)} %copy.42, bf16[2,128,256]{2,1,0:T(8,128)(2,1)S(1)} %get-tuple-element.153, bf16[16,128,256]{2,1,0:T(8,128)(2,1)} %get-tuple-element.179, bf16[8,2,256,16,16]{2,4,3,1,0:T(8,128)(2,1)} %get-tuple-element.178), kind=kOutput, calls=%fused_computation.4.clone.1 | convolution fusion | flops 34603008 | bytes 1704960 | tf_op jit(solution)/shard_map/while/body/eval_jaxpr/while/body/eval_jaxpr/bgij,bjgc->bigc/dot_general | solution.py:76
  163.7 2.0 select_reduce_fusion.2
  167.0 1.5 concatenate.39
  168.4 3.7 %reshape.118 = f32[16,128,257]{2,1,0:T(8,128)S(1)} reshape(f32[16,32896]{1,0:T(8,128)} %concatenate.39) | data formatting | bytes 4210688 | tf_op jit(solution)/shard_map/while/body/eval_jaxpr/while/body/eval_jaxpr/reshape | solution.py:24
  172.5 2.3 %copy.28 = bf16[16,128,256]{2,1,0:T(8,128)(2,1)} copy(bf16[16,128,256]{1,2,0:T(8,128)(2,1)} %bitcast.16) | data formatting | bytes 2097152 | tf_op jit(solution)/shard_map/convert_element_type | solution.py:91
  174.8 6.9 %all-to-all-start.2 = ((bf16[16,128,256]{2,1,0:T(8,128)(2,1)}), bf16[16,128,256]{2,1,0:T(8,128)(2,1)S(1)}, u32[]{:S(2)}, u32[]{:S(2)}) async-start(bf16[16,128,256]{2,1,0:T(8,128)(2,1)} %copy.28), calls=%async_computation.2 | async-start | bytes 2097152 | tf_op jit(solution)/shard_map/all_to_all | solution.py:136
  181.7 5.0 %psum.7 = f32[16,128]{1,0:T(8,128)S(1)} all-reduce(f32[16,128]{1,0:T(8,128)S(1)} %reduce_sum.57), channel_id=1, replica_groups=mesh['dp'=2,'ctx'=16] {'dp'}, use_global_device_ids=true, to_apply=%region_9.10 | all-reduce | flops 2048 | bytes 16384 | tf_op jit(solution)/shard_map/psum | solution.py:139
  187.3 17.3 %all-to-all-done.2 = bf16[16,128,256]{2,1,0:T(8,128)(2,1)S(1)} async-done(((bf16[16,128,256]{2,1,0:T(8,128)(2,1)}), bf16[16,128,256]{2,1,0:T(8,128)(2,1)S(1)}, u32[]{:S(2)}, u32[]{:S(2)}) %all-to-all-start.2) | async-done | bytes 1048608 | tf_op jit(solution)/shard_map/all_to_all | solution.py:136
  205.3 1.3 copy.30
  (85 shorter events, 33.6 us)
Async XLA Ops:
  0.6 40.9 %copy-start = (f32[256,128]{1,0:T(8,128)S(1)}, f32[256,128]{1,0:T(8,128)}, u32[]{:S(2)}) copy-start(f32[256,128]{1,0:T(8,128)} %param.10) | copy-start | bytes 393220
  2.5 8.7 %copy-start.1 = (bf16[128,4096]{1,0:T(8,128)(2,1)S(1)}, bf16[128,4096]{1,0:T(8,128)(2,1)}, u32[]{:S(2)}) copy-start(bf16[128,4096]{1,0:T(8,128)(2,1)} %param.8) | copy-start | bytes 3145732
  3.8 30.3 %all-to-all-start = ((bf16[128,16,256]{0,2,1:T(8,128)(2,1)}), bf16[128,16,256]{0,2,1:T(8,128)(2,1)S(1)}, u32[]{:S(2)}, u32[]{:S(2)}) async-start(bf16[128,16,256]{0,2,1:T(8,128)(2,1)} %bitcast.7), calls=%async_computation | async-start | bytes 2097152 | tf_op jit(solution)/shard_map/all_to_all | solution.py:107
  11.2 29.8 %copy-start.2 = (s32[1,16]{1,0:T(1,128)S(1)}, s32[1,16]{1,0:T(1,128)}, u32[]{:S(2)}) copy-start(s32[1,16]{1,0:T(1,128)} %param.11) | copy-start | bytes 196
  34.1 29.8 %all-to-all-start.1 = ((bf16[128,16,256]{0,2,1:T(8,128)(2,1)}), bf16[128,16,256]{0,2,1:T(8,128)(2,1)S(1)}, u32[]{:S(2)}, u32[]{:S(2)}) async-start(bf16[128,16,256]{0,2,1:T(8,128)(2,1)} %bitcast.12), calls=%async_computation.1 | async-start | bytes 2097152 | tf_op jit(solution)/shard_map/all_to_all | solution.py:108
  174.8 29.8 %all-to-all-start.2 = ((bf16[16,128,256]{2,1,0:T(8,128)(2,1)}), bf16[16,128,256]{2,1,0:T(8,128)(2,1)S(1)}, u32[]{:S(2)}, u32[]{:S(2)}) async-start(bf16[16,128,256]{2,1,0:T(8,128)(2,1)} %copy.28), calls=%async_computation.2 | async-start | bytes 2097152 | tf_op jit(solution)/shard_map/all_to_all | solution.py:136
where the time goes:
time: 209 us; the launch traced here: 207 us
  local copies, waits for them, and re-layouts  73.2 us (35%)
  waiting for transfers between devices  52.4 us (25%)
  matrix products  37.3 us (18%)
  starting transfers between devices  21.1 us (10%)
  other arithmetic  16.5 us (8%)
  blocking collectives  5.01 us (2%)
    reshape x8, local copies, waits for them, and re-layouts, lag_sums(): skewed = flattened.reshape(tile_count, 128, 257)  29.6 us
    all_to_all x1, waiting for transfers between devices, shards(): lax.all_to_all(mixed_grad, 'ctx', split_axis=1, concat_axis=0, tiled=True)  21.6 us
    dot_general x8, matrix products, per_block(): jnp.einsum('bgij,bjgc->bigc', kernel, mixed_block, preferred_element_type...  21.2 us
    all_to_all x1, waiting for transfers between devices, shards(): lax.all_to_all(down_all.reshape(total_rows, panel_width), 'ctx', split_ax...  17.3 us
    dot_general x8, matrix products, per_block(): jnp.einsum('bigc,bjgc->bgij', mixed_block[:, :128], input_block, preferre...  16.2 us
    all_to_all x1, waiting for transfers between devices, shards(): lax.all_to_all(conv_input, 'ctx', split_axis=1, concat_axis=0, tiled=True)  13.5 us
    concatenate x8, local copies, waits for them, and re-layouts, lag_sums(): jnp.concatenate([flattened, jnp.zeros((tile_count, 128), product.dtype)],...  11.9 us
    while x8, local copies, waits for them, and re-layouts  9.75 us
  transfers between devices with their start and end apart: 3, of which 3 were waited for; matrix products, arithmetic and copies ran while one was open for 5% of the time, Pallas kernels for 0%

commit v1 on v0

v1 whole, which is shorter than its diff:
```python
import functools

import jax
import jax.numpy as jnp
from jax import lax
from jax.experimental import pallas as pl
from jax.experimental.pallas import tpu as pltpu
from jax.sharding import PartitionSpec as P

GROUP = 16
FILT = 128
TILE = 256
HALF = 128
PAIRS = HALF // GROUP
BIG = 1 << 30
F32 = jnp.float32
BF16 = jnp.bfloat16


def document_masks(lens_ref, base, backwards):
    row = lax.broadcasted_iota(jnp.int32, (FILT, HALF), 0)
    if backwards:
        row = FILT - 1 - row
    column = lax.broadcasted_iota(jnp.int32, (FILT, HALF), 1)
    end_of = jnp.full((FILT, HALF), BIG, jnp.int32)
    end = -base
    for k in range(lens_ref.shape[1]):
        end = end + lens_ref[0, k]
        end_of = jnp.minimum(end_of, jnp.where(row < end, end, BIG))
    own = (column >= row) & (column < end_of)
    cross = (column < row) & (column + FILT < end_of)
    return own, cross


def lane_group():
    lane = lax.broadcasted_iota(jnp.int32, (FILT, TILE), 1)
    return (lane % HALF) // GROUP


def two_halves(rows):
    lane = lax.broadcasted_iota(jnp.int32, (FILT, TILE), 1)
    zero = jnp.zeros_like(rows)
    return jnp.concatenate([jnp.where(lane < HALF, rows, zero), jnp.where(lane >= HALF, rows, zero)], axis=0)


def split_groups(rows):
    which = lane_group()
    zero = jnp.zeros_like(rows)
    return jnp.concatenate([jnp.where(which == p, rows, zero) for p in range(PAIRS)], axis=0)


def lag_sums(products, mask):
    out = []
    for h in range(2):
        part = products[:, h * HALF : (h + 1) * HALF].reshape(PAIRS, FILT, HALF) * mask[None]
        part = pltpu.roll(part.reshape(PAIRS * FILT, HALF), 1, 1, stride=1, stride_axis=0)
        out.append(jnp.sum(part.reshape(PAIRS, FILT, HALF), axis=1))
    return jnp.concatenate(out, axis=0)


def pick_groups(stacked):
    which = lane_group()
    out = stacked[:FILT]
    for p in range(1, PAIRS):
        out = jnp.where(which == p, stacked[p * FILT : (p + 1) * FILT], out)
    return out


def circulants(taps):
    rows = jnp.broadcast_to(taps[:, None, :], (PAIRS, FILT, HALF)).reshape(PAIRS * FILT, HALF)
    return pltpu.roll(rows, 0, 1, stride=1, stride_axis=0)


def correlate(x_back, mixed_two):
    return lax.dot_general(split_groups(x_back), mixed_two, (((1,), (1,)), ((), ())), preferred_element_type=F32)


def backwards_rows(rows):
    i = lax.broadcasted_iota(jnp.int32, (FILT, FILT), 0)
    j = lax.broadcasted_iota(jnp.int32, (FILT, FILT), 1)
    flip = (i + j == FILT - 1).astype(BF16)
    return jnp.dot(flip, rows, preferred_element_type=F32).astype(BF16)


def own_kernel(lens_ref, place_ref, mixed_ref, x_ref, taps_ref, lag_ref, down_ref, cross_ref, xb_ref, mask_ref):
    @pl.when(pl.program_id(0) == 0)
    def _():
        base = place_ref[0] * FILT
        own, cross = document_masks(lens_ref, base, False)
        mask_ref[0] = own.astype(F32)
        mask_ref[1] = cross.astype(F32)
        own_back, _ = document_masks(lens_ref, base, True)
        mask_ref[2] = own_back.astype(F32)

    mixed_two = two_halves(mixed_ref[...])
    x_back = backwards_rows(x_ref[...])
    xb_ref[...] = x_back
    lag_ref[...] = lag_sums(correlate(x_back, mixed_two), mask_ref[2])
    taps = taps_ref[...].astype(BF16).astype(F32)
    bands = [circulants(taps[h * PAIRS : (h + 1) * PAIRS]).reshape(PAIRS, FILT, HALF) for h in range(2)]
    for h in range(2):
        cross_ref[:, h * HALF : (h + 1) * HALF] = (bands[h] * mask_ref[1][None]).astype(BF16).reshape(PAIRS * FILT, HALF)
    own_band = jnp.concatenate(
        [(band * mask_ref[0][None]).astype(BF16).reshape(PAIRS * FILT, HALF) for band in bands], axis=1
    )
    down_ref[...] = pick_groups(jnp.dot(own_band, mixed_two, preferred_element_type=F32))


def own_part(lens, place, mixed, x, taps):
    channels = x.shape[1]
    tiles = channels // TILE
    groups = channels // GROUP
    smem = pl.BlockSpec(memory_space=pltpu.SMEM)
    wide = pl.BlockSpec((FILT, TILE), lambda t: (0, t))
    return pl.pallas_call(
        own_kernel,
        grid=(tiles,),
        in_specs=[smem, smem, wide, wide, pl.BlockSpec((2 * PAIRS, FILT), lambda t: (t, 0))],
        out_specs=[
            pl.BlockSpec((2 * PAIRS, FILT), lambda t: (t, 0)),
            wide,
            pl.BlockSpec((PAIRS * FILT, TILE), lambda t: (t, 0)),
            wide,
        ],
        out_shape=[
            jax.ShapeDtypeStruct((groups, FILT), F32),
            jax.ShapeDtypeStruct((FILT, channels), F32),
            jax.ShapeDtypeStruct((tiles * PAIRS * FILT, TILE), BF16),
            jax.ShapeDtypeStruct((FILT, channels), BF16),
        ],
        scratch_shapes=[pltpu.VMEM((3, FILT, HALF), F32)],
        compiler_params=pltpu.CompilerParams(vmem_limit_bytes=24 << 20),
        cost_estimate=pl.CostEstimate(flops=2 * 2 * FILT * TILE * TILE * tiles * PAIRS, bytes_accessed=16 << 20, transcendentals=0),
        name="own_part",
    )(lens, place, mixed, x, taps)


def lag_kernel(lens_ref, place_ref, halo_ref, xb_ref, lag_ref, out_ref):
    _, mask = document_masks(lens_ref, place_ref[0] * FILT, True)
    mask = mask.astype(F32)
    for t in range(halo_ref.shape[1] // TILE):
        lanes = slice(t * TILE, (t + 1) * TILE)
        rows = slice(t * 2 * PAIRS, (t + 1) * 2 * PAIRS)
        sums = lag_sums(correlate(xb_ref[:, lanes], two_halves(halo_ref[:, lanes])), mask)
        out_ref[rows] = lag_ref[rows] + sums


def lag_part(lens, place, halo, x_back, lag, piece):
    width = halo.shape[1]
    rows = width // GROUP
    smem = pl.BlockSpec(memory_space=pltpu.SMEM)
    return pl.pallas_call(
        lag_kernel,
        grid=(1,),
        in_specs=[
            smem,
            smem,
            pl.BlockSpec((FILT, width), lambda i: (0, 0)),
            pl.BlockSpec((FILT, width), lambda i: (0, piece)),
            pl.BlockSpec((rows, FILT), lambda i: (piece, 0)),
        ],
        out_specs=pl.BlockSpec((rows, FILT), lambda i: (0, 0)),
        out_shape=jax.ShapeDtypeStruct((rows, FILT), F32),
        compiler_params=pltpu.CompilerParams(vmem_limit_bytes=24 << 20),
        cost_estimate=pl.CostEstimate(flops=2 * FILT * TILE * width * PAIRS, bytes_accessed=2 << 20, transcendentals=0),
        name="lag_part",
    )(lens, place, halo, x_back, lag)


def down_kernel(*refs):
    halo_refs, (cross_ref, down_ref, out_ref) = refs[:-3], refs[-3:]
    pieces = len(halo_refs)
    here = pl.program_id(0) // (pl.num_programs(0) // pieces)
    halo = halo_refs[0][...]
    for k in range(1, pieces):
        halo = jnp.where(here == k, halo_refs[k][...], halo)
    picked = pick_groups(jnp.dot(cross_ref[...], two_halves(halo), preferred_element_type=F32))
    out_ref[...] = (down_ref[...] + picked).astype(BF16)


def down_part(halos, cross_band, down):
    channels = down.shape[1]
    tiles = channels // TILE
    each = tiles // len(halos)
    wide = pl.BlockSpec((FILT, TILE), lambda t: (0, t))
    return pl.pallas_call(
        down_kernel,
        grid=(tiles,),
        in_specs=[
            pl.BlockSpec((FILT, TILE), functools.partial(lambda k, t: (0, jnp.clip(t - k * each, 0, each - 1)), k))
            for k in range(len(halos))
        ]
        + [pl.BlockSpec((PAIRS * FILT, TILE), lambda t: (t, 0)), wide],
        out_specs=wide,
        out_shape=jax.ShapeDtypeStruct((FILT, channels), BF16),
        compiler_params=pltpu.CompilerParams(vmem_limit_bytes=24 << 20),
        cost_estimate=pl.CostEstimate(flops=2 * FILT * TILE * TILE * tiles * PAIRS, bytes_accessed=12 << 20, transcendentals=0),
        name="down_part",
    )(*halos, cross_band, down)


def shards(pieces, gate_branch, conv_input, grad_output, filter_taps, document_lengths):
    local_rows, channels = gate_branch.shape
    ctx_count = lax.axis_size("ctx")
    dp_count = lax.axis_size("dp")
    grad_scale = (1.0 * GROUP * dp_count * local_rows * ctx_count) ** (-0.5)
    place = lax.axis_index("ctx").astype(jnp.int32).reshape(1)
    mixed = (grad_output.astype(F32) * gate_branch.astype(F32)).astype(BF16)
    width = channels // pieces
    back = [(i, i - 1) for i in range(1, ctx_count)]
    halos = [lax.ppermute(mixed[:, k * width : (k + 1) * width], "ctx", back) for k in range(pieces)]
    lag, down, cross_band, x_back = own_part(document_lengths, place, mixed, conv_input, filter_taps)
    lags = [lag_part(document_lengths, place, halos[k], x_back, lag, k) for k in range(pieces)]
    partial = jnp.concatenate(lags * dp_count, axis=0).reshape(dp_count * ctx_count, -1, FILT)
    shared = lax.all_to_all(partial, ("dp", "ctx"), 0, 0, tiled=True)
    filter_grad = jnp.sum(shared, axis=0) * grad_scale
    grad_input = down_part(halos, cross_band, down)
    return grad_input, filter_grad


def solution(mesh):
    rows = P(("dp", "ctx"), None)
    return jax.shard_map(
        functools.partial(shards, 2),
        mesh=mesh,
        in_specs=(rows, rows, rows, P(), P("dp", None)),
        out_specs=(rows, P("ctx", None)),
        check_vma=False,
    )
```

time: 209 us -> 56.2 us (0.27)
  local copies, waits for them, and re-layouts: 73.2 us -> 8.87 us
  waiting for transfers between devices: 52.4 us -> 0.01 us
  matrix products: 37.3 us -> 0 us
  Pallas kernels: 0 us -> 30.1 us
  other arithmetic: 16.5 us -> 3.17 us
  starting transfers between devices: 21.1 us -> 12.2 us
  blocking collectives: 5.01 us -> 0 us
    all_to_all x3 -> x1, waiting for transfers between devices: 52.4 us -> 0.01 us  [shards(): shared = lax.all_to_all(partial, ('dp', 'ctx'), 0, 0, tiled=True)]
    dot_general x16 -> x0, matrix products: 37.3 us -> none  [the longest x8 21.2 us: per_block(): jnp.einsum('bgij,bjgc->bigc', kernel, mixed_block, preferred_element_type...]
    reshape x9 -> x0, local copies, waits for them, and re-layouts: 32.7 us -> none  [the longest x8 29.6 us: lag_sums(): skewed = flattened.reshape(tile_count, 128, 257)]
    pallas_call x0 -> x4, Pallas kernels: none -> 30.1 us  [the longest x1 12.1 us: own_part(): pl.pallas_call(own_kernel, grid=(tiles,), in_specs=[smem, smem, wide, wid...]
    concatenate x10 -> x0, local copies, waits for them, and re-layouts: 12 us -> none  [the longest x8 11.9 us: lag_sums(): jnp.concatenate([flattened, jnp.zeros((tile_count, 128), product.dtype)],...]
    all_to_all x3 -> x1, starting transfers between devices: 21.1 us -> 9.68 us  [shards(): shared = lax.all_to_all(partial, ('dp', 'ctx'), 0, 0, tiled=True)]
    while x8 -> x0, local copies, waits for them, and re-layouts: 9.75 us -> none
    squeeze x8 -> x0, local copies, waits for them, and re-layouts: 7.79 us -> none  [per_group(): return lax.map(per_block, (keep_down, keep_lag, mixed_part, input_part))]
  transfers between devices with their start and end apart: 3 -> 3, of which waited for: 3 -> 0; matrix products, arithmetic and copies ran while one was open for 5% -> 0% of each run, Pallas kernels for 0% -> 48%
where the time goes in v1:
time: 56.2 us; the launch traced here: 55.2 us
  Pallas kernels  30.1 us (54%)
  starting transfers between devices  12.2 us (22%)
  local copies, waits for them, and re-layouts  8.87 us (16%)
  other arithmetic  3.17 us (6%)
  between operations  0.75 us (1%)
    pallas_call x1, Pallas kernels, own_part(): pl.pallas_call(own_kernel, grid=(tiles,), in_specs=[smem, smem, wide, wid...  12.1 us
    pallas_call x1, Pallas kernels, down_part(): pl.pallas_call(down_kernel, grid=(tiles,), in_specs=[pl.BlockSpec((FILT,...  10.8 us
    all_to_all x1, starting transfers between devices, shards(): shared = lax.all_to_all(partial, ('dp', 'ctx'), 0, 0, tiled=True)  9.68 us
    unnamed x10, local copies, waits for them, and re-layouts  7.83 us
    pallas_call x2, Pallas kernels, lag_part(): pl.pallas_call(lag_kernel, grid=(1,), in_specs=[smem, smem, pl.BlockSpec(...  7.19 us
    ppermute x2, starting transfers between devices, shards(): lax.ppermute(mixed[:, k * width:(k + 1) * width], 'ctx', back)  2.57 us
    convert_element_type x1, other arithmetic, shards(): mixed = (grad_output.astype(F32) * gate_branch.astype(F32)).astype(BF16)  1.82 us
  transfers between devices with their start and end apart: 3, of which 0 were waited for; matrix products, arithmetic and copies ran while one was open for 0% of the time, Pallas kernels for 48%

profile of v1, /device:TPU:0, one launch (start us, length us, event | category | flops | bytes accessed | tf_op | source)
XLA Modules:
  0.0 55.2 jit_solution(17128084482143081923)
XLA Ops:
  0.6 0.0 copy-start.4
  0.6 0.0 copy-start.3
  0.7 1.8 %multiply_convert_fusion.mixed_ref = bf16[128,4096]{1,0:T(8,128)(2,1)S(1)} fusion(bf16[128,4096]{1,0:T(8,128)(2,1)} %param.5, bf16[128,4096]{1,0:T(8,128)(2,1)} %param.7), kind=kLoop, calls=%fused_computation | loop fusion | flops 2097152 | bytes 3145728 | tf_op jit(solution)/shard_map/convert_element_type | solution.py:208
  2.5 1.0 %fusion = (bf16[128,2048]{1,0:T(8,128)(2,1)}, bf16[128,2048]{1,0:T(8,128)(2,1)}) fusion(bf16[128,4096]{1,0:T(8,128)(2,1)S(1)} %multiply_convert_fusion.mixed_ref), kind=kLoop, calls=%fused_computation.3 | loop fusion | bytes 2097152 | tf_op jit(solution)/shard_map/slice | solution.py:211
  3.5 1.3 %collective-permute-start.1 = (bf16[128,2048]{1,0:T(8,128)(2,1)}, bf16[128,2048]{1,0:T(8,128)(2,1)}, u32[]{:S(2)}, u32[]{:S(2)}) collective-permute-start(bf16[128,2048]{1,0:T(8,128)(2,1)} %get-tuple-element.10), channel_id=1, source_target_pairs={{1,0},{2,1},{3,2},{4,3},{5,4},{6,5},{7,6},{8,7},{9,8},{10,9},{11,1... | collective-permute-start | bytes 1572872 | tf_op jit(solution)/shard_map/ppermute | solution.py:211
  4.8 1.3 %collective-permute-start = (bf16[128,2048]{1,0:T(8,128)(2,1)}, bf16[128,2048]{1,0:T(8,128)(2,1)}, u32[]{:S(2)}, u32[]{:S(2)}) collective-permute-start(bf16[128,2048]{1,0:T(8,128)(2,1)} %get-tuple-element.11), channel_id=1, source_target_pairs={{1,0},{2,1},{3,2},{4,3},{5,4},{6,5},{7,6},{8,7},{9,8},{10,9},{11,1... | collective-permute-start | bytes 1572872 | tf_op jit(solution)/shard_map/ppermute | solution.py:211
  6.1 0.0 copy-done.4
  6.1 0.0 copy-done.3
  6.1 0.0 copy-start.2
  6.1 1.2 %copy-done.2 = bf16[128,4096]{1,0:T(8,128)(2,1)S(1)} copy-done((bf16[128,4096]{1,0:T(8,128)(2,1)S(1)}, bf16[128,4096]{1,0:T(8,128)(2,1)}, u32[]{:S(2)}) %copy-start.2) | copy-done | bytes 1048600
  7.4 12.1 %own_part.1 = (f32[256,128]{1,0:T(8,128)S(1)}, f32[128,4096]{1,0:T(8,128)S(1)}, bf16[16384,256]{1,0:T(8,128)(2,1)S(1)}, bf16[128,4096]{1,0:T(8,128)(2,1)S(1)}) custom-call(s32[1,16]{1,0:T(1,128)S(1)} %copy-done.4, s32[1]{0:T(128)} %bitcast.place_ref, bf16[128,4096]{1,0:T(8,128)(2,1)S(1)} %multiply_convert_fusion.mixed_ref, bf16[128,4096]{1,0:T(8,128)(2,1)S(1)} %copy-done.2, ...), custom_call_target="tpu_custom_call" | custom-call | flops 4294967296 | bytes 16777216 | tf_op jit(solution)/shard_map/own_part/pallas_call | solution.py:115
  19.5 0.0 copy-start
  19.5 3.2 %copy-done = bf16[16384,256]{1,0:T(8,128)(2,1)} copy-done((bf16[16384,256]{1,0:T(8,128)(2,1)}, bf16[16384,256]{1,0:T(8,128)(2,1)S(1)}, u32[]{:S(2)}) %copy-start) | copy-done | bytes 8388632
  22.7 0.0 collective-permute-done.1.refs_1_.halo_ref
  22.7 3.6 %lag_part.3 = f32[128,128]{1,0:T(8,128)S(1)} custom-call(s32[1,16]{1,0:T(1,128)S(1)} %copy-done.4, s32[1]{0:T(128)} %bitcast.place_ref, bf16[128,2048]{1,0:T(8,128)(2,1)} %collective-permute-done.1.refs_1_.halo_ref, bf16[128,4096]{1,0:T(8,128)(2,1)S(1)} %get-tuple-element.8.xb_ref, f32[256,128]{1,0:T(8,128)S(1)} %get-tuple-element.9.lag_ref), custom_call_target="tpu_custom_call" | custom-call | flops 1073741824 | bytes 2097152 | tf_op jit(solution)/shard_map/lag_part/pallas_call | solution.py:152
  26.3 0.0 collective-permute-done.refs_0_.halo_ref
  26.4 3.6 %lag_part.2 = f32[128,128]{1,0:T(8,128)S(1)} custom-call(s32[1,16]{1,0:T(1,128)S(1)} %copy-done.4, s32[1]{0:T(128)} %bitcast.place_ref, bf16[128,2048]{1,0:T(8,128)(2,1)} %collective-permute-done.refs_0_.halo_ref, bf16[128,4096]{1,0:T(8,128)(2,1)S(1)} %get-tuple-element.8.xb_ref, f32[256,128]{1,0:T(8,128)S(1)} %get-tuple-element.9.lag_ref), custom_call_target="tpu_custom_call" | custom-call | flops 1073741824 | bytes 2097152 | tf_op jit(solution)/shard_map/lag_part/pallas_call | solution.py:152
  30.0 0.7 %pad_maximum_fusion = f32[512,128]{1,0:T(8,128)} fusion(f32[128,128]{1,0:T(8,128)S(1)} %lag_part.3, f32[128,128]{1,0:T(8,128)S(1)} %lag_part.2), kind=kLoop, calls=%fused_computation.1 | loop fusion | flops 196608 | bytes 393216 | tf_op jit(solution)/shard_map/concatenate | solution.py:214
  30.7 9.7 %all-to-all-start = ((f32[32,16,128]{2,1,0:T(8,128)}), f32[32,16,128]{2,1,0:T(8,128)S(1)}, u32[]{:S(2)}, u32[]{:S(2)}) async-start(f32[32,16,128]{2,1,0:T(8,128)} %bitcast.1), calls=%async_computation | async-start | bytes 524288 | tf_op jit(solution)/shard_map/all_to_all | solution.py:215
  40.4 0.0 copy-start.1
  40.4 3.4 %copy-done.1 = bf16[16384,256]{1,0:T(8,128)(2,1)S(1)} copy-done((bf16[16384,256]{1,0:T(8,128)(2,1)S(1)}, bf16[16384,256]{1,0:T(8,128)(2,1)}, u32[]{:S(2)}) %copy-start.1) | copy-done | bytes 8388632
  43.7 10.8 %down_part.1 = bf16[128,4096]{1,0:T(8,128)(2,1)} custom-call(bf16[128,2048]{1,0:T(8,128)(2,1)} %collective-permute-done.refs_0_.halo_ref, bf16[128,2048]{1,0:T(8,128)(2,1)} %collective-permute-done.1.refs_1_.halo_ref, bf16[16384,256]{1,0:T(8,128)(2,1)S(1)} %copy-done.1, f32[128,4096]{1,0:T(8,128)S(1)} %get-tuple-element.7.refs_3_), custom_call_target="tpu_custom_call" | custom-call | flops 2147483648 | bytes 12582912 | tf_op jit(solution)/shard_map/down_part/pallas_call | solution.py:186
  54.5 0.0 all-to-all-done
  54.6 0.6 %broadcast_multiply_fusion = f32[16,128]{1,0:T(8,128)} fusion(f32[16,128]{1,0:T(8,128)S(1)} %reduce_sum.9), kind=kLoop, calls=%fused_computation.2 | loop fusion | flops 2048 | bytes 16384 | tf_op jit(solution)/shard_map/mul | solution.py:216
  (1 shorter events, 0.0 us)
Async XLA Ops:
  0.6 5.5 %copy-start.4 = (s32[1,16]{1,0:T(1,128)S(1)}, s32[1,16]{1,0:T(1,128)}, u32[]{:S(2)}) copy-start(s32[1,16]{1,0:T(1,128)} %lens_ref.5) | copy-start | bytes 196
  0.6 5.5 %copy-start.3 = (f32[256,128]{1,0:T(8,128)S(1)}, f32[256,128]{1,0:T(8,128)}, u32[]{:S(2)}) copy-start(f32[256,128]{1,0:T(8,128)} %taps_ref.1) | copy-start | bytes 393220
  3.5 19.2 %collective-permute-start.1 = (bf16[128,2048]{1,0:T(8,128)(2,1)}, bf16[128,2048]{1,0:T(8,128)(2,1)}, u32[]{:S(2)}, u32[]{:S(2)}) collective-permute-start(bf16[128,2048]{1,0:T(8,128)(2,1)} %get-tuple-element.10), channel_id=1, source_target_pairs={{1,0},{2,1},{3,2},{4,3},{5,4},{6,5},{7,6},{8,7},{9,8},{10,9},{11,1... | collective-permute-start | bytes 1572872 | tf_op jit(solution)/shard_map/ppermute | solution.py:211
  4.8 21.5 %collective-permute-start = (bf16[128,2048]{1,0:T(8,128)(2,1)}, bf16[128,2048]{1,0:T(8,128)(2,1)}, u32[]{:S(2)}, u32[]{:S(2)}) collective-permute-start(bf16[128,2048]{1,0:T(8,128)(2,1)} %get-tuple-element.11), channel_id=1, source_target_pairs={{1,0},{2,1},{3,2},{4,3},{5,4},{6,5},{7,6},{8,7},{9,8},{10,9},{11,1... | collective-permute-start | bytes 1572872 | tf_op jit(solution)/shard_map/ppermute | solution.py:211
  6.1 1.2 %copy-start.2 = (bf16[128,4096]{1,0:T(8,128)(2,1)S(1)}, bf16[128,4096]{1,0:T(8,128)(2,1)}, u32[]{:S(2)}) copy-start(bf16[128,4096]{1,0:T(8,128)(2,1)} %x_ref.1) | copy-start | bytes 3145732
  19.5 3.2 %copy-start = (bf16[16384,256]{1,0:T(8,128)(2,1)}, bf16[16384,256]{1,0:T(8,128)(2,1)S(1)}, u32[]{:S(2)}) copy-start(bf16[16384,256]{1,0:T(8,128)(2,1)S(1)} %get-tuple-element.6.refs_2_) | copy-start | bytes 25165828
  30.7 23.9 %all-to-all-start = ((f32[32,16,128]{2,1,0:T(8,128)}), f32[32,16,128]{2,1,0:T(8,128)S(1)}, u32[]{:S(2)}, u32[]{:S(2)}) async-start(f32[32,16,128]{2,1,0:T(8,128)} %bitcast.1), calls=%async_computation | async-start | bytes 524288 | tf_op jit(solution)/shard_map/all_to_all | solution.py:215
  40.4 3.4 %copy-start.1 = (bf16[16384,256]{1,0:T(8,128)(2,1)S(1)}, bf16[16384,256]{1,0:T(8,128)(2,1)}, u32[]{:S(2)}) copy-start(bf16[16384,256]{1,0:T(8,128)(2,1)} %copy-done) | copy-start | bytes 25165828

commit v2 on v1

v2 whole, which is shorter than its diff:
```python
import functools

import jax
import jax.numpy as jnp
from jax import lax
from jax.experimental import pallas as pl
from jax.experimental.pallas import tpu as pltpu
from jax.sharding import PartitionSpec as P

GROUP = 16
FILT = 128
TILE = 256
HALF = 128
PAIRS = HALF // GROUP
BLOCK = 32
STEPS = FILT // BLOCK
BIG = 1 << 30
F32 = jnp.float32
BF16 = jnp.bfloat16
VMEM = pl.BlockSpec(memory_space=pltpu.VMEM)
SMEM = pl.BlockSpec(memory_space=pltpu.SMEM)


def iotas(shape):
    return lax.broadcasted_iota(jnp.int32, shape, 0), lax.broadcasted_iota(jnp.int32, shape, 1)


def own_mask(lens_ref, base, step, backwards):
    b, k = iotas((BLOCK, HALF))
    if backwards:
        b = BLOCK - 1 - b
    row = b + BLOCK * step
    limit = jnp.full((BLOCK, HALF), FILT, jnp.int32)
    end = -base
    for n in range(lens_ref.shape[1]):
        end = end + lens_ref[0, n]
        limit = jnp.minimum(limit, jnp.where(row < end, end, BIG))
    return row + ((k - b) & (FILT - 1)) < limit


def span(lens_ref, base):
    first, count = jnp.int32(-BIG), jnp.int32(BIG)
    end = -base
    for n in range(lens_ref.shape[1]):
        end = end + lens_ref[0, n]
        inside = end < FILT
        first = jnp.where(inside, end, first)
        count = jnp.where(inside, count, jnp.minimum(count, end - FILT))
    return first, count


def cross_fold(backwards):
    b, k = iotas((BLOCK, HALF))
    if backwards:
        b = BLOCK - 1 - b
    return (k >= BLOCK) | (k < b)


def halves(rows):
    lane = lax.broadcasted_iota(jnp.int32, rows.shape, 1)
    zero = jnp.zeros_like(rows)
    return jnp.where(lane < HALF, rows, zero), jnp.where(lane >= HALF, rows, zero)


def turned(rows, step):
    if step == 0:
        return rows
    return jnp.concatenate([rows[BLOCK * step :], rows[: BLOCK * step]], axis=0)


def turned_cross(rows, step):
    parts = [rows[BLOCK * step : BLOCK * (step + 1)]]
    if step < STEPS - 1:
        parts.append(jnp.zeros((BLOCK * (STEPS - 1 - step), rows.shape[1]), rows.dtype))
    if step > 0:
        parts.append(rows[: BLOCK * step])
    return jnp.concatenate(parts, axis=0)


def split_groups(rows):
    which = (lax.broadcasted_iota(jnp.int32, rows.shape, 1) % HALF) // GROUP
    zero = jnp.zeros_like(rows)
    return jnp.concatenate([jnp.where(which == p, rows, zero) for p in range(PAIRS)], axis=0)


def pick_groups(stacked):
    which = (lax.broadcasted_iota(jnp.int32, (BLOCK, TILE), 1) % HALF) // GROUP
    out = stacked[:BLOCK]
    for p in range(1, PAIRS):
        out = jnp.where(which == p, stacked[p * BLOCK : (p + 1) * BLOCK], out)
    return out


def correlate(x_back, step, stacked):
    at = STEPS - 1 - step
    rows = split_groups(x_back[BLOCK * at : BLOCK * (at + 1)])
    return lax.dot_general(rows, stacked, (((1,), (1,)), ((), ())), preferred_element_type=F32)


def lag_sums(total):
    out = []
    for h in range(2):
        for p in range(PAIRS):
            part = total[p * BLOCK : (p + 1) * BLOCK, h * HALF : (h + 1) * HALF]
            part = pltpu.roll(part, HALF - BLOCK + 1, 1, stride=1, stride_axis=0)
            out.append(jnp.sum(part, axis=0, keepdims=True))
    return jnp.concatenate(out, axis=0)


def bands(taps):
    out = []
    for h in range(2):
        groups = []
        for p in range(h * PAIRS, (h + 1) * PAIRS):
            rows = jnp.broadcast_to(taps[p : p + 1], (BLOCK, HALF))
            groups.append(pltpu.roll(rows, 0, 1, stride=1, stride_axis=0))
        out.append(jnp.concatenate(groups, axis=0))
    return jnp.concatenate(out, axis=1)


def backwards_rows(rows):
    i, j = iotas((FILT, FILT))
    flip = (i + j == FILT - 1).astype(BF16)
    return jnp.dot(flip, rows, preferred_element_type=F32).astype(BF16)


def tiled(mask):
    return jnp.concatenate([mask] * PAIRS, axis=0)


def own_kernel(pieces, *refs):
    lens_ref, place_ref = refs[:2]
    mixed_refs = refs[2 : 2 + pieces]
    x_ref, taps_ref, lag_ref, down_ref, band_ref, xb_ref, back_ref, ahead_ref = refs[2 + pieces :]
    base = place_ref[0] * FILT
    for step in range(STEPS):
        back_ref[step] = own_mask(lens_ref, base, step, True).astype(F32)
        ahead = own_mask(lens_ref, base, step, False).astype(F32).astype(BF16)
        ahead_ref[step] = jnp.concatenate([ahead, ahead], axis=1)
    fold = cross_fold(False).astype(F32).astype(BF16)
    fold = tiled(jnp.concatenate([fold, fold], axis=1))
    first, _ = span(lens_ref, base)
    row, _ = iotas((FILT, TILE))
    keep = (FILT - 1 - row >= first).astype(F32).astype(BF16)
    at = 0
    for mixed_ref in mixed_refs:
        for t in range(mixed_ref.shape[1] // TILE):
            lanes = slice(at * TILE, (at + 1) * TILE)
            groups = slice(at * 2 * PAIRS, (at + 1) * 2 * PAIRS)
            stack = slice(at * PAIRS * BLOCK, (at + 1) * PAIRS * BLOCK)
            at += 1
            low, high = halves(mixed_ref[:, t * TILE : (t + 1) * TILE])
            x_back = backwards_rows(x_ref[:, lanes])
            xb_ref[:, lanes] = x_back * keep
            band = bands(taps_ref[groups].astype(BF16).astype(F32)).astype(BF16)
            band_ref[stack] = band * fold
            total = None
            for step in range(STEPS):
                stacked = jnp.concatenate([turned(low, step), turned(high, step)], axis=0)
                product = correlate(x_back, step, stacked).reshape(PAIRS, BLOCK, TILE)
                mask = back_ref[step]
                product = product * jnp.concatenate([mask, mask], axis=1)[None]
                total = product if total is None else total + product
                down = jnp.dot(band * tiled(ahead_ref[step]), stacked, preferred_element_type=F32)
                down_ref[BLOCK * step : BLOCK * (step + 1), lanes] = pick_groups(down)
            lag_ref[groups] = lag_sums(total.reshape(PAIRS * BLOCK, TILE))


def own_part(lens, place, mixed, x, taps):
    channels = x.shape[1]
    tiles = channels // TILE
    return pl.pallas_call(
        functools.partial(own_kernel, len(mixed)),
        in_specs=[SMEM, SMEM] + [VMEM] * (len(mixed) + 2),
        out_specs=[VMEM] * 4,
        out_shape=[
            jax.ShapeDtypeStruct((channels // GROUP, FILT), F32),
            jax.ShapeDtypeStruct((FILT, channels), F32),
            jax.ShapeDtypeStruct((tiles * PAIRS * BLOCK, TILE), BF16),
            jax.ShapeDtypeStruct((FILT, channels), BF16),
        ],
        scratch_shapes=[pltpu.VMEM((STEPS, BLOCK, HALF), F32), pltpu.VMEM((STEPS, BLOCK, TILE), BF16)],
        compiler_params=pltpu.CompilerParams(vmem_limit_bytes=24 << 20),
        cost_estimate=pl.CostEstimate(flops=4 * FILT * TILE * TILE * tiles * PAIRS, bytes_accessed=8 << 20, transcendentals=0),
        name="own_part",
    )(lens, place, *mixed, x, taps)


def next_rows(count, halo):
    row, _ = iotas(halo.shape)
    return halves(halo * (row < count).astype(F32).astype(BF16))


def lag_kernel(first_group, scale, copies, *refs):
    lens_ref, place_ref, halo_ref, xb_ref, lag_ref = refs[:5]
    out_ref = refs[-1]
    earlier = refs[5:-1]
    _, count = span(lens_ref, place_ref[0] * FILT)
    fold = cross_fold(True).astype(F32)
    fold = tiled(jnp.concatenate([fold, fold], axis=1))
    if earlier:
        done = earlier[0][...]
        for c in range(copies):
            out_ref[c, :first_group] = done
    for t in range(halo_ref.shape[1] // TILE):
        low, high = next_rows(count, halo_ref[:, t * TILE : (t + 1) * TILE])
        at = first_group * GROUP + t * TILE
        total = None
        for step in range(STEPS):
            stacked = jnp.concatenate([turned_cross(low, step), turned_cross(high, step)], axis=0)
            product = correlate(xb_ref[:, at : at + TILE], step, stacked)
            total = product if total is None else total + product
        rows = first_group + t * 2 * PAIRS
        sums = (lag_ref[rows : rows + 2 * PAIRS] + lag_sums(total * fold)) * scale
        if copies:
            for c in range(copies):
                out_ref[c, rows : rows + 2 * PAIRS] = sums
        else:
            out_ref[rows : rows + 2 * PAIRS] = sums


def lag_part(lens, place, halo, x_back, lag, first_group, scale, copies, earlier):
    width = halo.shape[1]
    rows = first_group + width // GROUP
    shape = (copies, rows, FILT) if copies else (rows, FILT)
    return pl.pallas_call(
        functools.partial(lag_kernel, first_group, scale, copies),
        in_specs=[SMEM, SMEM] + [VMEM] * (3 + len(earlier)),
        out_specs=VMEM,
        out_shape=jax.ShapeDtypeStruct(shape, F32),
        compiler_params=pltpu.CompilerParams(vmem_limit_bytes=16 << 20),
        cost_estimate=pl.CostEstimate(flops=2 * FILT * TILE * width * PAIRS, bytes_accessed=2 << 20, transcendentals=0),
        name="lag_part",
    )(lens, place, halo, x_back, lag, *earlier)


def down_kernel(pieces, *refs):
    lens_ref, place_ref = refs[:2]
    halo_refs = refs[2 : 2 + pieces]
    band_ref, down_ref, out_ref, rows_ref, sems = refs[2 + pieces :]
    first, count = span(lens_ref, place_ref[0] * FILT)
    row, _ = iotas((BLOCK, TILE))
    at = 0
    copies = []
    for halo_ref in halo_refs:
        for t in range(halo_ref.shape[1] // TILE):
            lanes = slice(at * TILE, (at + 1) * TILE)
            low, high = next_rows(count, halo_ref[:, t * TILE : (t + 1) * TILE])
            band = band_ref[at * PAIRS * BLOCK : (at + 1) * PAIRS * BLOCK]
            for step in range(STEPS):
                stacked = jnp.concatenate([turned_cross(low, step), turned_cross(high, step)], axis=0)
                picked = pick_groups(jnp.dot(band, stacked, preferred_element_type=F32))
                rows = slice(BLOCK * step, BLOCK * (step + 1))
                picked = jnp.where(row + BLOCK * step >= first, picked, 0.0)
                rows_ref[rows, lanes] = (down_ref[rows, lanes] + picked).astype(BF16)
            copy = pltpu.make_async_copy(rows_ref.at[:, lanes], out_ref.at[:, lanes], sems.at[at])
            copy.start()
            copies.append(copy)
            at += 1
    for copy in copies:
        copy.wait()


def down_part(lens, place, halos, band, down):
    channels = down.shape[1]
    tiles = channels // TILE
    return pl.pallas_call(
        functools.partial(down_kernel, len(halos)),
        in_specs=[SMEM, SMEM] + [VMEM] * (len(halos) + 2),
        out_specs=pl.BlockSpec(memory_space=pl.ANY),
        out_shape=jax.ShapeDtypeStruct((FILT, channels), BF16),
        scratch_shapes=[pltpu.VMEM((FILT, channels), BF16), pltpu.SemaphoreType.DMA((tiles,))],
        compiler_params=pltpu.CompilerParams(vmem_limit_bytes=16 << 20),
        cost_estimate=pl.CostEstimate(flops=2 * FILT * TILE * TILE * tiles * PAIRS, bytes_accessed=4 << 20, transcendentals=0),
        name="down_part",
    )(lens, place, *halos, band, down)


def shards(gate_branch, conv_input, grad_output, filter_taps, document_lengths):
    local_rows, channels = gate_branch.shape
    ctx_count = lax.axis_size("ctx")
    dp_count = lax.axis_size("dp")
    grad_scale = (1.0 * GROUP * dp_count * local_rows * ctx_count) ** (-0.5)
    place = lax.axis_index("ctx").astype(jnp.int32).reshape(1)
    cuts = [0, channels // 2, channels]
    back = [(i, i - 1) for i in range(1, ctx_count)]
    mixed, halos = [], []
    for low, high in zip(cuts, cuts[1:]):
        gate, grad = gate_branch[:, low:high], grad_output[:, low:high]
        mixed.append((grad.astype(F32) * gate.astype(F32)).astype(BF16))
        halos.append(lax.ppermute(mixed[-1], "ctx", back))
    lag, down, band, x_back = own_part(document_lengths, place, mixed, conv_input, filter_taps)
    sums = []
    for k in range(len(halos)):
        copies = dp_count if k == len(halos) - 1 else 0
        sums = [lag_part(document_lengths, place, halos[k], x_back, lag, cuts[k] // GROUP, grad_scale, copies, sums)]
    partial = sums[0].reshape(dp_count * ctx_count, -1, FILT)
    shared = lax.all_to_all(partial, ("dp", "ctx"), 0, 0, tiled=True)
    filter_grad = jnp.sum(shared, axis=0)
    grad_input = down_part(document_lengths, place, halos, band, down)
    return grad_input, filter_grad


def solution(mesh):
    rows = P(("dp", "ctx"), None)
    return jax.shard_map(
        shards,
        mesh=mesh,
        in_specs=(rows, rows, rows, P(), P("dp", None)),
        out_specs=(rows, P("ctx", None)),
        check_vma=False,
    )
```

time: 56.2 us -> 39.4 us (0.70); the launches traced: 55.2 us -> 39.1 us
  Pallas kernels: 30.1 us -> 16.4 us
  local copies, waits for them, and re-layouts: 8.87 us -> 3.2 us
  waiting for transfers between devices: 0.01 us -> 3.15 us
  starting transfers between devices: 12.2 us -> 12.9 us
    pallas_call x4, Pallas kernels: 30.1 us -> 16.4 us  [the longest x1 7.86 us: own_part(): pl.pallas_call(functools.partial(own_kernel, len(mixed)), in_specs=[SMEM,...]
    unnamed x10 -> x14, local copies, waits for them, and re-layouts: 7.83 us -> 3.2 us
    all_to_all x1, waiting for transfers between devices: 0.01 us -> 3.14 us  [shards(): shared = lax.all_to_all(partial, ('dp', 'ctx'), 0, 0, tiled=True)]
    slice x1 -> x0, local copies, waits for them, and re-layouts: 1.04 us -> none  [shards(): mixed[:, k * width:(k + 1) * width]]
    concatenate x1 -> x0, other arithmetic: 0.71 us -> none  [shards(): jnp.concatenate(lags * dp_count, axis=0)]
    all_to_all x1, starting transfers between devices: 9.68 us -> 10.3 us  [shards(): shared = lax.all_to_all(partial, ('dp', 'ctx'), 0, 0, tiled=True)]
    mul x1 -> x0, other arithmetic: 0.6 us -> none  [shards(): filter_grad = jnp.sum(shared, axis=0) * grad_scale]
    reduce_sum x1, other arithmetic: 0.04 us -> 0.63 us  [shards(): filter_grad = jnp.sum(shared, axis=0)]
  transfers between devices with their start and end apart: 3 -> 3, of which waited for: 0 -> 1; matrix products, arithmetic and copies ran while one was open for 0% -> 0% of each run, Pallas kernels for 48% -> 35%
where the time goes in v2:
time: 39.4 us; the launch traced here: 39.1 us
  Pallas kernels  16.4 us (42%)
  starting transfers between devices  12.9 us (33%)
  local copies, waits for them, and re-layouts  3.2 us (8%)
  waiting for transfers between devices  3.15 us (8%)
  other arithmetic  2.63 us (7%)
  between operations  0.78 us (2%)
    all_to_all x1, starting transfers between devices, shards(): shared = lax.all_to_all(partial, ('dp', 'ctx'), 0, 0, tiled=True)  10.3 us
    pallas_call x1, Pallas kernels, own_part(): pl.pallas_call(functools.partial(own_kernel, len(mixed)), in_specs=[SMEM,...  7.86 us
    pallas_call x2, Pallas kernels, lag_part(): pl.pallas_call(functools.partial(lag_kernel, first_group, scale, copies),...  4.77 us
    pallas_call x1, Pallas kernels, down_part(): pl.pallas_call(functools.partial(down_kernel, len(halos)), in_specs=[SMEM...  3.77 us
    unnamed x14, local copies, waits for them, and re-layouts  3.2 us
    all_to_all x1, waiting for transfers between devices, shards(): shared = lax.all_to_all(partial, ('dp', 'ctx'), 0, 0, tiled=True)  3.14 us
    ppermute x2, starting transfers between devices, shards(): halos.append(lax.ppermute(mixed[-1], 'ctx', back))  2.58 us
    convert_element_type x1, other arithmetic, shards(): mixed.append((grad.astype(F32) * gate.astype(F32)).astype(BF16))  2 us
  transfers between devices with their start and end apart: 3, of which 1 were waited for; matrix products, arithmetic and copies ran while one was open for 0% of the time, Pallas kernels for 35%

profile of v2, /device:TPU:0, one launch (start us, length us, event | category | flops | bytes accessed | tf_op | source)
XLA Modules:
  0.0 39.1 jit_solution(13532710948316867979)
XLA Ops:
  0.6 0.0 copy-start
  0.6 0.0 copy-start.1
  0.7 0.0 copy-start.2
  0.7 2.0 %multiply_convert_fusion = (bf16[128,2048]{1,0:T(8,128)(2,1)S(1)}, bf16[128,2048]{1,0:T(8,128)(2,1)S(1)}) fusion(bf16[128,4096]{1,0:T(8,128)(2,1)} %param.5, bf16[128,4096]{1,0:T(8,128)(2,1)} %param.7), kind=kLoop, calls=%fused_computation | loop fusion | flops 2097152 | bytes 3145728 | tf_op jit(solution)/shard_map/convert_element_type | solution.py:290
  2.7 1.3 %collective-permute-start = (bf16[128,2048]{1,0:T(8,128)(2,1)S(1)}, bf16[128,2048]{1,0:T(8,128)(2,1)S(1)}, u32[]{:S(2)}, u32[]{:S(2)}) collective-permute-start(bf16[128,2048]{1,0:T(8,128)(2,1)S(1)} %get-tuple-element.11.refs_2_), channel_id=1, source_target_pairs={{1,0},{2,1},{3,2},{4,3},{5,4},{6,5},{7,6},{8,7},{9,8},{10,9},{11,1... | collective-permute-start | bytes 1572872 | tf_op jit(solution)/shard_map/ppermute | solution.py:291
  4.0 1.3 %collective-permute-start.1 = (bf16[128,2048]{1,0:T(8,128)(2,1)S(1)}, bf16[128,2048]{1,0:T(8,128)(2,1)S(1)}, u32[]{:S(2)}, u32[]{:S(2)}) collective-permute-start(bf16[128,2048]{1,0:T(8,128)(2,1)S(1)} %get-tuple-element.10.refs_3_), channel_id=1, source_target_pairs={{1,0},{2,1},{3,2},{4,3},{5,4},{6,5},{7,6},{8,7},{9,8},{10,9},{11,1... | collective-permute-start | bytes 1572872 | tf_op jit(solution)/shard_map/ppermute | solution.py:291
  5.3 0.0 copy-done
  5.3 0.0 copy-done.1
  5.3 0.0 copy-done.2
  5.3 7.9 %own_part.1 = (f32[256,128]{1,0:T(8,128)S(1)}, f32[128,4096]{1,0:T(8,128)S(1)}, bf16[4096,256]{1,0:T(8,128)(2,1)S(1)}, bf16[128,4096]{1,0:T(8,128)(2,1)S(1)}) custom-call(s32[1,16]{1,0:T(1,128)S(1)} %copy-done.2, s32[1]{0:T(128)} %bitcast.refs_1_, bf16[128,2048]{1,0:T(8,128)(2,1)S(1)} %get-tuple-element.11.refs_2_, ...), custom_call_target="tpu_custom_call" | custom-call | flops 4294967296 | bytes 8388608 | tf_op jit(solution)/shard_map/own_part/pallas_call | solution.py:172
  13.2 0.0 copy-start.3
  13.2 0.0 copy-start.5
  13.2 0.0 collective-permute-done.refs_2_
  13.2 2.0 %lag_part.2.refs_5_ = f32[128,128]{1,0:T(8,128)S(1)} custom-call(s32[1,16]{1,0:T(1,128)S(1)} %copy-done.2, s32[1]{0:T(128)} %bitcast.refs_1_, bf16[128,2048]{1,0:T(8,128)(2,1)S(1)} %collective-permute-done.refs_2_, bf16[128,4096]{1,0:T(8,128)(2,1)S(1)} %get-tuple-element.8.refs_3_, f32[256,128]{1,0:T(8,128)S(1)} %get-tuple-element.9.refs_4_), custom_call_target="tpu_custom_call" | custom-call | flops 1073741824 | bytes 2097152 | tf_op jit(solution)/shard_map/lag_part/pallas_call | solution.py:226
  15.2 0.0 collective-permute-done.1.refs_3_.refs_2_
  15.2 2.7 %lag_part.3 = f32[2,256,128]{2,1,0:T(8,128)} custom-call(s32[1,16]{1,0:T(1,128)S(1)} %copy-done.2, s32[1]{0:T(128)} %bitcast.refs_1_, bf16[128,2048]{1,0:T(8,128)(2,1)S(1)} %collective-permute-done.1.refs_3_.refs_2_, bf16[128,4096]{1,0:T(8,128)(2,1)S(1)} %get-tuple-element.8.refs_3_, f32[256,128]{1,0:T(8,128)S(1)} %get-tuple-element.9.refs_4_, ...), custom_call_target="tpu_custom_call" | custom-call | flops 1073741824 | bytes 2097152 | tf_op jit(solution)/shard_map/lag_part/pallas_call | solution.py:226
  18.0 0.0 copy-done.3
  18.0 0.0 copy-done.5
  18.0 10.3 %all-to-all-start = ((f32[32,16,128]{2,1,0:T(8,128)}), f32[32,16,128]{2,1,0:T(8,128)S(1)}, u32[]{:S(2)}, u32[]{:S(2)}) async-start(f32[32,16,128]{2,1,0:T(8,128)} %bitcast.1), calls=%async_computation | async-start | bytes 524288 | tf_op jit(solution)/shard_map/all_to_all | solution.py:298
  28.3 0.0 copy-start.4
  28.3 1.6 %copy-done.4 = f32[128,4096]{1,0:T(8,128)S(1)} copy-done((f32[128,4096]{1,0:T(8,128)S(1)}, f32[128,4096]{1,0:T(8,128)}, u32[]{:S(2)}) %copy-start.4) | copy-done | bytes 2097176
  29.9 0.0 copy-start.6
  29.9 1.6 %copy-done.6 = bf16[4096,256]{1,0:T(8,128)(2,1)S(1)} copy-done((bf16[4096,256]{1,0:T(8,128)(2,1)S(1)}, bf16[4096,256]{1,0:T(8,128)(2,1)}, u32[]{:S(2)}) %copy-start.6) | copy-done | bytes 2097176
  31.5 3.8 %down_part.1 = bf16[128,4096]{1,0:T(8,128)(2,1)} custom-call(s32[1,16]{1,0:T(1,128)S(1)} %copy-done.2, s32[1]{0:T(128)} %bitcast.refs_1_, bf16[128,2048]{1,0:T(8,128)(2,1)S(1)} %collective-permute-done.refs_2_, bf16[128,2048]{1,0:T(8,128)(2,1)S(1)} %collective-permute-done.1.refs_3_.refs_2_, bf16[4096,256]{1,0:T(8,128)(2,1)S(1)} %copy-done.6, ...), custom_call_target="tpu_custom_call" | custom-call | flops 2147483648 | bytes 4194304 | tf_op jit(solution)/shard_map/down_part/pallas_call | solution.py:267
  35.3 3.1 %all-to-all-done = f32[32,16,128]{2,1,0:T(8,128)S(1)} async-done(((f32[32,16,128]{2,1,0:T(8,128)}), f32[32,16,128]{2,1,0:T(8,128)S(1)}, u32[]{:S(2)}, u32[]{:S(2)}) %all-to-all-start) | async-done | bytes 262176 | tf_op jit(solution)/shard_map/all_to_all | solution.py:298
  38.4 0.6 %reduce_sum.9 = f32[16,128]{1,0:T(8,128)} reduce(f32[32,16,128]{2,1,0:T(8,128)S(1)} %all-to-all-done, f32[]{:T(128)} %constant.1.clone.1), dimensions={0}, to_apply=%region_0.0 | reduce | flops 63488 | bytes 270340 | tf_op jit(solution)/shard_map/reduce_sum | solution.py:299
Async XLA Ops:
  0.6 4.6 %copy-start = (bf16[128,4096]{1,0:T(8,128)(2,1)S(1)}, bf16[128,4096]{1,0:T(8,128)(2,1)}, u32[]{:S(2)}) copy-start(bf16[128,4096]{1,0:T(8,128)(2,1)} %refs_4_.1) | copy-start | bytes 3145732
  0.6 4.6 %copy-start.1 = (f32[256,128]{1,0:T(8,128)S(1)}, f32[256,128]{1,0:T(8,128)}, u32[]{:S(2)}) copy-start(f32[256,128]{1,0:T(8,128)} %refs_5_.1) | copy-start | bytes 393220
  0.7 4.6 %copy-start.2 = (s32[1,16]{1,0:T(1,128)S(1)}, s32[1,16]{1,0:T(1,128)}, u32[]{:S(2)}) copy-start(s32[1,16]{1,0:T(1,128)} %refs_0_.7) | copy-start | bytes 196
  2.7 10.5 %collective-permute-start = (bf16[128,2048]{1,0:T(8,128)(2,1)S(1)}, bf16[128,2048]{1,0:T(8,128)(2,1)S(1)}, u32[]{:S(2)}, u32[]{:S(2)}) collective-permute-start(bf16[128,2048]{1,0:T(8,128)(2,1)S(1)} %get-tuple-element.11.refs_2_), channel_id=1, source_target_pairs={{1,0},{2,1},{3,2},{4,3},{5,4},{6,5},{7,6},{8,7},{9,8},{10,9},{11,1... | collective-permute-start | bytes 1572872 | tf_op jit(solution)/shard_map/ppermute | solution.py:291
  4.0 11.3 %collective-permute-start.1 = (bf16[128,2048]{1,0:T(8,128)(2,1)S(1)}, bf16[128,2048]{1,0:T(8,128)(2,1)S(1)}, u32[]{:S(2)}, u32[]{:S(2)}) collective-permute-start(bf16[128,2048]{1,0:T(8,128)(2,1)S(1)} %get-tuple-element.10.refs_3_), channel_id=1, source_target_pairs={{1,0},{2,1},{3,2},{4,3},{5,4},{6,5},{7,6},{8,7},{9,8},{10,9},{11,1... | collective-permute-start | bytes 1572872 | tf_op jit(solution)/shard_map/ppermute | solution.py:291
  13.2 4.8 %copy-start.3 = (f32[128,4096]{1,0:T(8,128)}, f32[128,4096]{1,0:T(8,128)S(1)}, u32[]{:S(2)}) copy-start(f32[128,4096]{1,0:T(8,128)S(1)} %get-tuple-element.7.refs_5_) | copy-start | bytes 6291460
  13.2 4.8 %copy-start.5 = (bf16[4096,256]{1,0:T(8,128)(2,1)}, bf16[4096,256]{1,0:T(8,128)(2,1)S(1)}, u32[]{:S(2)}) copy-start(bf16[4096,256]{1,0:T(8,128)(2,1)S(1)} %get-tuple-element.6.refs_4_) | copy-start | bytes 6291460
  18.0 20.4 %all-to-all-start = ((f32[32,16,128]{2,1,0:T(8,128)}), f32[32,16,128]{2,1,0:T(8,128)S(1)}, u32[]{:S(2)}, u32[]{:S(2)}) async-start(f32[32,16,128]{2,1,0:T(8,128)} %bitcast.1), calls=%async_computation | async-start | bytes 524288 | tf_op jit(solution)/shard_map/all_to_all | solution.py:298
  28.3 1.6 %copy-start.4 = (f32[128,4096]{1,0:T(8,128)S(1)}, f32[128,4096]{1,0:T(8,128)}, u32[]{:S(2)}) copy-start(f32[128,4096]{1,0:T(8,128)} %copy-done.3) | copy-start | bytes 6291460
  29.9 1.6 %copy-start.6 = (bf16[4096,256]{1,0:T(8,128)(2,1)S(1)}, bf16[4096,256]{1,0:T(8,128)(2,1)}, u32[]{:S(2)}) copy-start(bf16[4096,256]{1,0:T(8,128)(2,1)} %copy-done.5) | copy-start | bytes 6291460

commit v3 on v2

v3 whole, which is shorter than its diff:
```python
import functools

import jax
import jax.numpy as jnp
from jax import lax
from jax.experimental import pallas as pl
from jax.experimental.pallas import tpu as pltpu
from jax.sharding import PartitionSpec as P

GROUP = 16
FILT = 128
TILE = 256
HALF = 128
PAIRS = HALF // GROUP
BLOCK = 32
STEPS = FILT // BLOCK
BIG = 1 << 30
F32 = jnp.float32
BF16 = jnp.bfloat16
SENT = jnp.bfloat16
VMEM = pl.BlockSpec(memory_space=pltpu.VMEM)
SMEM = pl.BlockSpec(memory_space=pltpu.SMEM)


def iotas(shape):
    return lax.broadcasted_iota(jnp.int32, shape, 0), lax.broadcasted_iota(jnp.int32, shape, 1)


def own_mask(lens_ref, base, step, backwards):
    b, k = iotas((BLOCK, HALF))
    if backwards:
        b = BLOCK - 1 - b
    row = b + BLOCK * step
    limit = jnp.full((BLOCK, HALF), FILT, jnp.int32)
    end = -base
    for n in range(lens_ref.shape[1]):
        end = end + lens_ref[0, n]
        limit = jnp.minimum(limit, jnp.where(row < end, end, BIG))
    return row + ((k - b) & (FILT - 1)) < limit


def span(lens_ref, base):
    first, count = jnp.int32(-BIG), jnp.int32(BIG)
    end = -base
    for n in range(lens_ref.shape[1]):
        end = end + lens_ref[0, n]
        inside = end < FILT
        first = jnp.where(inside, end, first)
        count = jnp.where(inside, count, jnp.minimum(count, end - FILT))
    return first, count


def cross_fold(backwards):
    b, k = iotas((BLOCK, HALF))
    if backwards:
        b = BLOCK - 1 - b
    return (k >= BLOCK) | (k < b)


def halves(rows):
    lane = lax.broadcasted_iota(jnp.int32, rows.shape, 1)
    zero = jnp.zeros_like(rows)
    return jnp.where(lane < HALF, rows, zero), jnp.where(lane >= HALF, rows, zero)


def turned(rows, step):
    if step == 0:
        return rows
    return jnp.concatenate([rows[BLOCK * step :], rows[: BLOCK * step]], axis=0)


def turned_cross(rows, step):
    parts = [rows[BLOCK * step : BLOCK * (step + 1)]]
    if step < STEPS - 1:
        parts.append(jnp.zeros((BLOCK * (STEPS - 1 - step), rows.shape[1]), rows.dtype))
    if step > 0:
        parts.append(rows[: BLOCK * step])
    return jnp.concatenate(parts, axis=0)


def split_groups(rows):
    which = (lax.broadcasted_iota(jnp.int32, rows.shape, 1) % HALF) // GROUP
    zero = jnp.zeros_like(rows)
    return jnp.concatenate([jnp.where(which == p, rows, zero) for p in range(PAIRS)], axis=0)


def pick_groups(stacked):
    which = (lax.broadcasted_iota(jnp.int32, (BLOCK, TILE), 1) % HALF) // GROUP
    out = stacked[:BLOCK]
    for p in range(1, PAIRS):
        out = jnp.where(which == p, stacked[p * BLOCK : (p + 1) * BLOCK], out)
    return out


def correlate(x_back, step, stacked):
    at = STEPS - 1 - step
    rows = split_groups(x_back[BLOCK * at : BLOCK * (at + 1)])
    return lax.dot_general(rows, stacked, (((1,), (1,)), ((), ())), preferred_element_type=F32)


def lag_sums(total):
    out = []
    for h in range(2):
        for p in range(PAIRS):
            part = total[p * BLOCK : (p + 1) * BLOCK, h * HALF : (h + 1) * HALF]
            part = pltpu.roll(part, HALF - BLOCK + 1, 1, stride=1, stride_axis=0)
            out.append(jnp.sum(part, axis=0, keepdims=True))
    return jnp.concatenate(out, axis=0)


def bands(taps):
    out = []
    for h in range(2):
        groups = []
        for p in range(h * PAIRS, (h + 1) * PAIRS):
            rows = jnp.broadcast_to(taps[p : p + 1], (BLOCK, HALF))
            groups.append(pltpu.roll(rows, 0, 1, stride=1, stride_axis=0))
        out.append(jnp.concatenate(groups, axis=0))
    return jnp.concatenate(out, axis=1)


def backwards_rows(rows):
    i, j = iotas((FILT, FILT))
    flip = (i + j == FILT - 1).astype(BF16)
    return jnp.dot(flip, rows, preferred_element_type=F32).astype(BF16)


def tiled(mask):
    return jnp.concatenate([mask] * PAIRS, axis=0)


def own_kernel(pieces, *refs):
    lens_ref, place_ref = refs[:2]
    mixed_refs = refs[2 : 2 + pieces]
    x_ref, lag_ref, xb_ref, keep_ref, mask_ref, back_ref = refs[2 + pieces :]
    base = place_ref[0] * FILT
    first, count = span(lens_ref, base)
    row, _ = iotas((FILT, TILE))
    keep_ref[0] = (FILT - 1 - row >= first).astype(F32).astype(BF16)
    keep_ref[1] = (row < count).astype(F32).astype(BF16)
    row, _ = iotas((BLOCK, HALF))
    for step in range(STEPS):
        back = own_mask(lens_ref, base, step, True).astype(F32)
        back_ref[step] = jnp.concatenate([back, back], axis=1)
        ahead = own_mask(lens_ref, base, step, False)
        cross = cross_fold(False) & (row + BLOCK * step >= first)
        masks = [mask.astype(F32).astype(BF16) for mask in (ahead, ahead, cross, cross)]
        mask_ref[step] = jnp.concatenate(masks, axis=1)
    tiles = []
    for k in range(pieces):
        for t in range(mixed_refs[k].shape[1] // TILE):
            tiles.append((len(tiles), k, t))
    for at, _, _ in tiles:
        lanes = slice(at * TILE, (at + 1) * TILE)
        xb_ref[:, lanes] = backwards_rows(x_ref[:, lanes])
    for at, k, t in tiles:
        groups = slice(at * 2 * PAIRS, (at + 1) * 2 * PAIRS)
        low, high = halves(mixed_refs[k][:, t * TILE : (t + 1) * TILE])
        x_back = xb_ref[:, at * TILE : (at + 1) * TILE]
        total = None
        for step in range(STEPS):
            stacked = jnp.concatenate([turned(low, step), turned(high, step)], axis=0)
            product = correlate(x_back, step, stacked).reshape(PAIRS, BLOCK, TILE) * back_ref[step][None]
            total = product if total is None else total + product
        lag_ref[groups] = lag_sums(total.reshape(PAIRS * BLOCK, TILE))


def own_part(lens, place, mixed, x):
    channels = x.shape[1]
    pieces = len(mixed)
    return pl.pallas_call(
        functools.partial(own_kernel, pieces),
        in_specs=[SMEM, SMEM] + [VMEM] * (pieces + 1),
        out_specs=[VMEM] * 4,
        out_shape=[
            jax.ShapeDtypeStruct((channels // GROUP, FILT), F32),
            jax.ShapeDtypeStruct((FILT, channels), BF16),
            jax.ShapeDtypeStruct((2, FILT, TILE), BF16),
            jax.ShapeDtypeStruct((STEPS, BLOCK, 2 * TILE), BF16),
        ],
        scratch_shapes=[pltpu.VMEM((STEPS, BLOCK, TILE), F32)],
        compiler_params=pltpu.CompilerParams(vmem_limit_bytes=16 << 20),
        cost_estimate=pl.CostEstimate(flops=2 * FILT * TILE * channels * PAIRS, bytes_accessed=4 << 20, transcendentals=0),
        name="own_part",
    )(lens, place, *mixed, x)


def lag_kernel(first_group, scale, copies, *refs):
    keep_ref, halo_ref, xb_ref, lag_ref = refs[:4]
    out_ref = refs[-1]
    earlier = refs[4:-1]
    fold = cross_fold(True).astype(F32)
    fold = tiled(jnp.concatenate([fold, fold], axis=1))
    if earlier:
        done = earlier[0][...].astype(out_ref.dtype)
        for c in range(copies):
            out_ref[c, :first_group] = done
    for t in range(halo_ref.shape[1] // TILE):
        low, high = halves(halo_ref[:, t * TILE : (t + 1) * TILE] * keep_ref[1])
        at = first_group * GROUP + t * TILE
        x_back = xb_ref[:, at : at + TILE] * keep_ref[0]
        total = None
        for step in range(STEPS):
            stacked = jnp.concatenate([turned_cross(low, step), turned_cross(high, step)], axis=0)
            product = correlate(x_back, step, stacked)
            total = product if total is None else total + product
        rows = first_group + t * 2 * PAIRS
        sums = (lag_ref[rows : rows + 2 * PAIRS] + lag_sums(total * fold)) * scale
        if copies:
            for c in range(copies):
                out_ref[c, rows : rows + 2 * PAIRS] = sums.astype(out_ref.dtype)
        else:
            out_ref[rows : rows + 2 * PAIRS] = sums


def lag_part(keep, halo, x_back, lag, first_group, scale, copies, earlier):
    width = halo.shape[1]
    rows = first_group + width // GROUP
    shape = jax.ShapeDtypeStruct((copies, rows, FILT), SENT) if copies else jax.ShapeDtypeStruct((rows, FILT), F32)
    return pl.pallas_call(
        functools.partial(lag_kernel, first_group, scale, copies),
        in_specs=[VMEM] * (4 + len(earlier)),
        out_specs=VMEM,
        out_shape=shape,
        compiler_params=pltpu.CompilerParams(vmem_limit_bytes=16 << 20),
        cost_estimate=pl.CostEstimate(flops=2 * FILT * TILE * width * PAIRS, bytes_accessed=2 << 20, transcendentals=0),
        name="lag_part",
    )(keep, halo, x_back, lag, *earlier)


def down_kernel(pieces, *refs):
    keep_ref, mask_ref, taps_ref = refs[:3]
    mixed_refs = refs[3 : 3 + pieces]
    halo_refs = refs[3 + pieces : 3 + 2 * pieces]
    out_ref, band_ref, rows_ref, sems = refs[3 + 2 * pieces :]
    tiles = []
    for k in range(pieces):
        for t in range(mixed_refs[k].shape[1] // TILE):
            tiles.append((len(tiles), k, t))
    for at, _, _ in tiles:
        taps = taps_ref[at * 2 * PAIRS : (at + 1) * 2 * PAIRS].astype(BF16).astype(F32)
        band_ref[at * PAIRS * BLOCK : (at + 1) * PAIRS * BLOCK] = bands(taps).astype(BF16)
    copies = []
    for at, k, t in tiles:
        lanes = slice(t * TILE, (t + 1) * TILE)
        low, high = halves(mixed_refs[k][:, lanes])
        next_low, next_high = halves(halo_refs[k][:, lanes] * keep_ref[1])
        band = band_ref[at * PAIRS * BLOCK : (at + 1) * PAIRS * BLOCK]
        band = jnp.concatenate([band, band], axis=1)
        for step in range(STEPS):
            stacked = [turned(low, step), turned(high, step), turned_cross(next_low, step), turned_cross(next_high, step)]
            stacked = jnp.concatenate(stacked, axis=0)
            product = jnp.dot(band * tiled(mask_ref[step]), stacked, preferred_element_type=F32)
            rows_ref[BLOCK * step : BLOCK * (step + 1), at * TILE : (at + 1) * TILE] = pick_groups(product).astype(BF16)
        lanes = slice(at * TILE, (at + 1) * TILE)
        copy = pltpu.make_async_copy(rows_ref.at[:, lanes], out_ref.at[:, lanes], sems.at[at])
        copy.start()
        copies.append(copy)
    for copy in copies:
        copy.wait()


def down_part(keep, masks, taps, mixed, halos):
    pieces = len(mixed)
    channels = taps.shape[0] * GROUP
    tiles = channels // TILE
    return pl.pallas_call(
        functools.partial(down_kernel, pieces),
        in_specs=[VMEM] * (3 + 2 * pieces),
        out_specs=pl.BlockSpec(memory_space=pl.ANY),
        out_shape=jax.ShapeDtypeStruct((FILT, channels), BF16),
        scratch_shapes=[
            pltpu.VMEM((tiles * PAIRS * BLOCK, TILE), BF16),
            pltpu.VMEM((FILT, channels), BF16),
            pltpu.SemaphoreType.DMA((tiles,)),
        ],
        compiler_params=pltpu.CompilerParams(vmem_limit_bytes=16 << 20),
        cost_estimate=pl.CostEstimate(flops=4 * FILT * TILE * channels * PAIRS, bytes_accessed=4 << 20, transcendentals=0),
        name="down_part",
    )(keep, masks, taps, *mixed, *halos)


def shards(gate_branch, conv_input, grad_output, filter_taps, document_lengths):
    local_rows, channels = gate_branch.shape
    ctx_count = lax.axis_size("ctx")
    dp_count = lax.axis_size("dp")
    grad_scale = (1.0 * GROUP * dp_count * local_rows * ctx_count) ** (-0.5)
    place = lax.axis_index("ctx").astype(jnp.int32).reshape(1)
    cuts = [0, channels * 5 // 8, channels]
    back = [(i, i - 1) for i in range(1, ctx_count)]
    mixed, halos = [], []
    gate, grad = gate_branch, grad_output
    for low, high in zip(cuts, cuts[1:]):
        if mixed:
            gate, grad, mixed[-1] = lax.optimization_barrier((gate, grad, mixed[-1]))
        mixed.append((grad[:, low:high].astype(F32) * gate[:, low:high].astype(F32)).astype(BF16))
        halos.append(lax.ppermute(mixed[-1], "ctx", back))
    pieces = len(mixed)
    lag, x_back, keep, masks = own_part(document_lengths, place, mixed, conv_input)
    sums = []
    for k in range(pieces):
        copies = dp_count if k == pieces - 1 else 0
        sums = [lag_part(keep, halos[k], x_back, lag, cuts[k] // GROUP, grad_scale, copies, sums)]
    partial = sums[0].reshape(dp_count * ctx_count, -1, FILT)
    shared = lax.all_to_all(partial, ("dp", "ctx"), 0, 0, tiled=True)
    filter_grad = jnp.sum(shared.astype(F32), axis=0)
    grad_input = down_part(keep, masks, filter_taps, mixed, halos)
    return grad_input, filter_grad


def solution(mesh):
    rows = P(("dp", "ctx"), None)
    return jax.shard_map(
        shards,
        mesh=mesh,
        in_specs=(rows, rows, rows, P(), P("dp", None)),
        out_specs=(rows, P("ctx", None)),
        check_vma=False,
    )
```

time: 39.4 us -> 35.9 us (0.911)
  Pallas kernels: 16.4 us -> 12.6 us
  starting transfers between devices: 12.9 us -> 16.2 us
  local copies, waits for them, and re-layouts: 3.2 us -> 0.02 us
  other arithmetic: 2.63 us -> 3.28 us
    unnamed x14 -> x6, local copies, waits for them, and re-layouts: 3.2 us -> 0.02 us
    all_to_all x1, starting transfers between devices: 10.3 us -> 13.5 us  [shards(): shared = lax.all_to_all(partial, ('dp', 'ctx'), 0, 0, tiled=True)]
    pallas_call x2, Pallas kernels: 11.6 us -> 9.03 us  [the longest x1 5.38 us: down_part(): pl.pallas_call(functools.partial(down_kernel, pieces), in_specs=[VMEM] *...]
    pallas_call x2, Pallas kernels: 4.77 us -> 3.58 us  [lag_part(): pl.pallas_call(functools.partial(lag_kernel, first_group, scale, copies),...]
    convert_element_type x1 -> x2, other arithmetic: 2 us -> 2.65 us  [shards(): (grad[:, low:high].astype(F32) * gate[:, low:high].astype(F32)).astype(BF16)]
  transfers between devices with their start and end apart: 3 -> 3, of which waited for: 1 -> 1; matrix products, arithmetic and copies ran while one was open for 0% -> 3% of each run, Pallas kernels for 35% -> 30%
where the time goes in v3:
time: 35.9 us; the launch traced here: 35.7 us
  starting transfers between devices  16.2 us (45%)
  Pallas kernels  12.6 us (35%)
  other arithmetic  3.28 us (9%)
  waiting for transfers between devices  2.84 us (8%)
  between operations  0.75 us (2%)
    all_to_all x1, starting transfers between devices, shards(): shared = lax.all_to_all(partial, ('dp', 'ctx'), 0, 0, tiled=True)  13.5 us
    pallas_call x1, Pallas kernels, down_part(): pl.pallas_call(functools.partial(down_kernel, pieces), in_specs=[VMEM] *...  5.38 us
    pallas_call x1, Pallas kernels, own_part(): pl.pallas_call(functools.partial(own_kernel, pieces), in_specs=[SMEM, SME...  3.65 us
    pallas_call x2, Pallas kernels, lag_part(): pl.pallas_call(functools.partial(lag_kernel, first_group, scale, copies),...  3.58 us
    all_to_all x1, waiting for transfers between devices, shards(): shared = lax.all_to_all(partial, ('dp', 'ctx'), 0, 0, tiled=True)  2.83 us
    ppermute x2, starting transfers between devices, shards(): halos.append(lax.ppermute(mixed[-1], 'ctx', back))  2.72 us
    convert_element_type x2, other arithmetic, shards(): (grad[:, low:high].astype(F32) * gate[:, low:high].astype(F32)).astype(BF16)  2.65 us
  transfers between devices with their start and end apart: 3, of which 1 were waited for; matrix products, arithmetic and copies ran while one was open for 3% of the time, Pallas kernels for 30%

profile of v3, /device:TPU:0, one launch (start us, length us, event | category | flops | bytes accessed | tf_op | source)
XLA Modules:
  0.0 35.7 jit_solution(12929372318842328136)
XLA Ops:
  0.6 1.4 %multiply_convert_fusion.refs_2_.refs_3_ = bf16[128,2560]{1,0:T(8,128)(2,1)S(1)} fusion(bf16[128,4096]{1,0:T(8,128)(2,1)} %param.5, bf16[128,4096]{1,0:T(8,128)(2,1)} %param.7), kind=kLoop, calls=%fused_computation | loop fusion | flops 1310720 | bytes 1966080 | tf_op jit(solution)/shard_map/convert_element_type | solution.py:296
  2.1 0.0 copy-start
  2.1 0.0 copy-start.2
  2.1 1.4 %collective-permute-start = (bf16[128,2560]{1,0:T(8,128)(2,1)S(1)}, bf16[128,2560]{1,0:T(8,128)(2,1)S(1)}, u32[]{:S(2)}, u32[]{:S(2)}) collective-permute-start(bf16[128,2560]{1,0:T(8,128)(2,1)S(1)} %multiply_convert_fusion.refs_2_.refs_3_), channel_id=1, source_target_pairs={{1,0},{2,1},{3,2},{4,3},{5,4},{6,5},{7,6},{8,7},{9,8},{10,9},{11,1... | collective-permute-start | bytes 1966088 | tf_op jit(solution)/shard_map/ppermute | solution.py:297
  3.5 1.2 %multiply_convert_fusion.1.refs_3_.refs_4_ = bf16[128,1536]{1,0:T(8,128)(2,1)S(1)} fusion(bf16[128,4096]{1,0:T(8,128)(2,1)} %param.5, bf16[128,4096]{1,0:T(8,128)(2,1)} %param.7), kind=kLoop, calls=%fused_computation.1 | loop fusion | flops 786432 | bytes 1179648 | tf_op jit(solution)/shard_map/convert_element_type | solution.py:296
  4.7 1.3 %collective-permute-start.1 = (bf16[128,1536]{1,0:T(8,128)(2,1)S(1)}, bf16[128,1536]{1,0:T(8,128)(2,1)S(1)}, u32[]{:S(2)}, u32[]{:S(2)}) collective-permute-start(bf16[128,1536]{1,0:T(8,128)(2,1)S(1)} %multiply_convert_fusion.1.refs_3_.refs_4_), channel_id=1, source_target_pairs={{1,0},{2,1},{3,2},{4,3},{5,4},{6,5},{7,6},{8,7},{9,8},{10,9},{11,1... | collective-permute-start | bytes 1179656 | tf_op jit(solution)/shard_map/ppermute | solution.py:297
  6.0 0.0 copy-done
  6.1 0.0 copy-done.2
  6.1 3.7 %own_part.1 = (f32[256,128]{1,0:T(8,128)S(1)}, bf16[128,4096]{1,0:T(8,128)(2,1)S(1)}, bf16[2,128,256]{2,1,0:T(8,128)(2,1)S(1)}, bf16[4,32,512]{2,1,0:T(8,128)(2,1)S(1)}) custom-call(s32[1,16]{1,0:T(1,128)S(1)} %copy-done.2, s32[1]{0:T(128)} %bitcast.refs_1_, bf16[128,2560]{1,0:T(8,128)(2,1)S(1)} %multiply_convert_fusion.refs_2_.refs_3_, ...), custom_call_target="tpu_custom_call" | custom-call | flops 2147483648 | bytes 4194304 | tf_op jit(solution)/shard_map/own_part/pallas_call | solution.py:171
  9.7 0.0 collective-permute-done.refs_5_.refs_1_
  9.7 1.7 %lag_part.2.refs_4_ = f32[160,128]{1,0:T(8,128)S(1)} custom-call(bf16[2,128,256]{2,1,0:T(8,128)(2,1)S(1)} %get-tuple-element.12.refs_0_, bf16[128,2560]{1,0:T(8,128)(2,1)S(1)} %collective-permute-done.refs_5_.refs_1_, bf16[128,4096]{1,0:T(8,128)(2,1)S(1)} %get-tuple-element.14.refs_2_, f32[256,128]{1,0:T(8,128)S(1)} %get-tuple-element.15.refs_3_), custom_call_target="tpu_custom_call" | custom-call | flops 1342177280 | bytes 2097152 | tf_op jit(solution)/shard_map/lag_part/pallas_call | solution.py:220
  11.5 0.0 copy-start.1
  11.5 0.0 collective-permute-done.1.refs_6_.refs_1_
  11.5 1.8 %lag_part.3 = bf16[2,256,128]{2,1,0:T(8,128)(2,1)} custom-call(bf16[2,128,256]{2,1,0:T(8,128)(2,1)S(1)} %get-tuple-element.12.refs_0_, bf16[128,1536]{1,0:T(8,128)(2,1)S(1)} %collective-permute-done.1.refs_6_.refs_1_, bf16[128,4096]{1,0:T(8,128)(2,1)S(1)} %get-tuple-element.14.refs_2_, f32[256,128]{1,0:T(8,128)S(1)} %get-tuple-element.15.refs_3_, ...), custom_call_target="tpu_custom_call" | custom-call | flops 805306368 | bytes 2097152 | tf_op jit(solution)/shard_map/lag_part/pallas_call | solution.py:220
  13.3 13.5 %all-to-all-start = ((bf16[32,16,128]{2,1,0:T(8,128)(2,1)}), bf16[32,16,128]{2,1,0:T(8,128)(2,1)S(1)}, u32[]{:S(2)}, u32[]{:S(2)}) async-start(bf16[32,16,128]{2,1,0:T(8,128)(2,1)} %bitcast.1), calls=%async_computation | async-start | bytes 262144 | tf_op jit(solution)/shard_map/all_to_all | solution.py:305
  26.8 0.0 copy-done.1
  26.8 5.4 %down_part.1 = bf16[128,4096]{1,0:T(8,128)(2,1)} custom-call(bf16[2,128,256]{2,1,0:T(8,128)(2,1)S(1)} %get-tuple-element.12.refs_0_, bf16[4,32,512]{2,1,0:T(8,128)(2,1)S(1)} %get-tuple-element.13.refs_1_, f32[256,128]{1,0:T(8,128)S(1)} %copy-done.1, bf16[128,2560]{1,0:T(8,128)(2,1)S(1)} %multiply_convert_fusion.refs_2_.refs_3_, ...), custom_call_target="tpu_custom_call" | custom-call | flops 4294967296 | bytes 4194304 | tf_op jit(solution)/shard_map/down_part/pallas_call | solution.py:267
  32.2 2.8 %all-to-all-done = bf16[32,16,128]{2,1,0:T(8,128)(2,1)S(1)} async-done(((bf16[32,16,128]{2,1,0:T(8,128)(2,1)}), bf16[32,16,128]{2,1,0:T(8,128)(2,1)S(1)}, u32[]{:S(2)}, u32[]{:S(2)}) %all-to-all-start) | async-done | bytes 131104 | tf_op jit(solution)/shard_map/all_to_all | solution.py:305
  35.0 0.6 %convert_reduce_fusion = f32[16,128]{1,0:T(8,128)} fusion(bf16[32,16,128]{2,1,0:T(8,128)(2,1)S(1)} %all-to-all-done), kind=kLoop, calls=%fused_computation.2 | loop fusion | flops 129024 | bytes 139264 | tf_op jit(solution)/shard_map/reduce_sum | solution.py:306
Async XLA Ops:
  2.1 4.0 %copy-start = (bf16[128,4096]{1,0:T(8,128)(2,1)S(1)}, bf16[128,4096]{1,0:T(8,128)(2,1)}, u32[]{:S(2)}) copy-start(bf16[128,4096]{1,0:T(8,128)(2,1)} %refs_4_.1) | copy-start | bytes 3145732
  2.1 4.0 %copy-start.2 = (s32[1,16]{1,0:T(1,128)S(1)}, s32[1,16]{1,0:T(1,128)}, u32[]{:S(2)}) copy-start(s32[1,16]{1,0:T(1,128)} %refs_0_.1) | copy-start | bytes 196
  2.1 7.6 %collective-permute-start = (bf16[128,2560]{1,0:T(8,128)(2,1)S(1)}, bf16[128,2560]{1,0:T(8,128)(2,1)S(1)}, u32[]{:S(2)}, u32[]{:S(2)}) collective-permute-start(bf16[128,2560]{1,0:T(8,128)(2,1)S(1)} %multiply_convert_fusion.refs_2_.refs_3_), channel_id=1, source_target_pairs={{1,0},{2,1},{3,2},{4,3},{5,4},{6,5},{7,6},{8,7},{9,8},{10,9},{11,1... | collective-permute-start | bytes 1966088 | tf_op jit(solution)/shard_map/ppermute | solution.py:297
  4.7 6.8 %collective-permute-start.1 = (bf16[128,1536]{1,0:T(8,128)(2,1)S(1)}, bf16[128,1536]{1,0:T(8,128)(2,1)S(1)}, u32[]{:S(2)}, u32[]{:S(2)}) collective-permute-start(bf16[128,1536]{1,0:T(8,128)(2,1)S(1)} %multiply_convert_fusion.1.refs_3_.refs_4_), channel_id=1, source_target_pairs={{1,0},{2,1},{3,2},{4,3},{5,4},{6,5},{7,6},{8,7},{9,8},{10,9},{11,1... | collective-permute-start | bytes 1179656 | tf_op jit(solution)/shard_map/ppermute | solution.py:297
  11.5 15.3 %copy-start.1 = (f32[256,128]{1,0:T(8,128)S(1)}, f32[256,128]{1,0:T(8,128)}, u32[]{:S(2)}) copy-start(f32[256,128]{1,0:T(8,128)} %refs_2_.1) | copy-start | bytes 393220
  13.3 21.7 %all-to-all-start = ((bf16[32,16,128]{2,1,0:T(8,128)(2,1)}), bf16[32,16,128]{2,1,0:T(8,128)(2,1)S(1)}, u32[]{:S(2)}, u32[]{:S(2)}) async-start(bf16[32,16,128]{2,1,0:T(8,128)(2,1)} %bitcast.1), calls=%async_computation | async-start | bytes 262144 | tf_op jit(solution)/shard_map/all_to_all | solution.py:305

commit v4 on v3

--- a/solution.py
+++ b/solution.py
@@ -193,8 +193,11 @@
     fold = tiled(jnp.concatenate([fold, fold], axis=1))
     if earlier:
         done = earlier[0][...].astype(out_ref.dtype)
-        for c in range(copies):
-            out_ref[c, :first_group] = done
+        if copies:
+            for c in range(copies):
+                out_ref[c, :first_group] = done
+        else:
+            out_ref[:first_group] = done
     for t in range(halo_ref.shape[1] // TILE):
         low, high = halves(halo_ref[:, t * TILE : (t + 1) * TILE] * keep_ref[1])
         at = first_group * GROUP + t * TILE
@@ -286,12 +289,12 @@
     dp_count = lax.axis_size("dp")
     grad_scale = (1.0 * GROUP * dp_count * local_rows * ctx_count) ** (-0.5)
     place = lax.axis_index("ctx").astype(jnp.int32).reshape(1)
-    cuts = [0, channels * 5 // 8, channels]
+    cuts = [0, channels * 5 // 8, channels * 7 // 8, channels]
     back = [(i, i - 1) for i in range(1, ctx_count)]
     mixed, halos = [], []
     gate, grad = gate_branch, grad_output
     for low, high in zip(cuts, cuts[1:]):
-        if mixed:
+        if len(mixed) == 1:
             gate, grad, mixed[-1] = lax.optimization_barrier((gate, grad, mixed[-1]))
         mixed.append((grad[:, low:high].astype(F32) * gate[:, low:high].astype(F32)).astype(BF16))
         halos.append(lax.ppermute(mixed[-1], "ctx", back))

time: 35.9 us -> 35.7 us (level)
  starting transfers between devices: 16.2 us -> 14.6 us
  other arithmetic: 3.28 us -> 4.18 us
    all_to_all x1, starting transfers between devices: 13.5 us -> 10.6 us  [shards(): shared = lax.all_to_all(partial, ('dp', 'ctx'), 0, 0, tiled=True)]
    ppermute x2 -> x3, starting transfers between devices: 2.72 us -> 4.01 us  [shards(): halos.append(lax.ppermute(mixed[-1], 'ctx', back))]
    convert_element_type x2 -> x3, other arithmetic: 2.65 us -> 3.55 us  [shards(): (grad[:, low:high].astype(F32) * gate[:, low:high].astype(F32)).astype(BF16)]
    pallas_call x2 -> x3, Pallas kernels: 3.58 us -> 3.91 us  [lag_part(): pl.pallas_call(functools.partial(lag_kernel, first_group, scale, copies),...]
  transfers between devices with their start and end apart: 3 -> 4, of which waited for: 1 -> 1; matrix products, arithmetic and copies ran while one was open for 3% -> 6% of each run, Pallas kernels for 30% -> 33%
where the time goes in v4:
time: 35.7 us; the launch traced here: 35.4 us
  starting transfers between devices  14.6 us (41%)
  Pallas kernels  12.9 us (36%)
  other arithmetic  4.18 us (12%)
  waiting for transfers between devices  2.84 us (8%)
  between operations  0.77 us (2%)
    all_to_all x1, starting transfers between devices, shards(): shared = lax.all_to_all(partial, ('dp', 'ctx'), 0, 0, tiled=True)  10.6 us
    pallas_call x1, Pallas kernels, down_part(): pl.pallas_call(functools.partial(down_kernel, pieces), in_specs=[VMEM] *...  5.38 us
    ppermute x3, starting transfers between devices, shards(): halos.append(lax.ppermute(mixed[-1], 'ctx', back))  4.01 us
    pallas_call x3, Pallas kernels, lag_part(): pl.pallas_call(functools.partial(lag_kernel, first_group, scale, copies),...  3.91 us
    pallas_call x1, Pallas kernels, own_part(): pl.pallas_call(functools.partial(own_kernel, pieces), in_specs=[SMEM, SME...  3.66 us
    convert_element_type x3, other arithmetic, shards(): (grad[:, low:high].astype(F32) * gate[:, low:high].astype(F32)).astype(BF16)  3.55 us
    all_to_all x1, waiting for transfers between devices, shards(): shared = lax.all_to_all(partial, ('dp', 'ctx'), 0, 0, tiled=True)  2.84 us
  transfers between devices with their start and end apart: 4, of which 1 were waited for; matrix products, arithmetic and copies ran while one was open for 6% of the time, Pallas kernels for 33%

profile of v4, /device:TPU:0, one launch (start us, length us, event | category | flops | bytes accessed | tf_op | source)
XLA Modules:
  0.0 35.4 jit_solution(10466414881346260323)
XLA Ops:
  0.6 1.4 %multiply_convert_fusion.refs_2_.refs_3_ = bf16[128,2560]{1,0:T(8,128)(2,1)S(1)} fusion(bf16[128,4096]{1,0:T(8,128)(2,1)} %param.5, bf16[128,4096]{1,0:T(8,128)(2,1)} %param.7), kind=kLoop, calls=%fused_computation | loop fusion | flops 1310720 | bytes 1966080 | tf_op jit(solution)/shard_map/convert_element_type | solution.py:299
  2.1 0.0 copy-start
  2.1 0.0 copy-start.2
  2.1 1.4 %collective-permute-start = (bf16[128,2560]{1,0:T(8,128)(2,1)S(1)}, bf16[128,2560]{1,0:T(8,128)(2,1)S(1)}, u32[]{:S(2)}, u32[]{:S(2)}) collective-permute-start(bf16[128,2560]{1,0:T(8,128)(2,1)S(1)} %multiply_convert_fusion.refs_2_.refs_3_), channel_id=1, source_target_pairs={{1,0},{2,1},{3,2},{4,3},{5,4},{6,5},{7,6},{8,7},{9,8},{10,9},{11,1... | collective-permute-start | bytes 1966088 | tf_op jit(solution)/shard_map/ppermute | solution.py:300
  3.5 1.1 %multiply_convert_fusion.1.refs_3_.refs_4_ = bf16[128,1024]{1,0:T(8,128)(2,1)S(1)} fusion(bf16[128,4096]{1,0:T(8,128)(2,1)} %param.5, bf16[128,4096]{1,0:T(8,128)(2,1)} %param.7), kind=kLoop, calls=%fused_computation.1 | loop fusion | flops 524288 | bytes 786432 | tf_op jit(solution)/shard_map/convert_element_type | solution.py:299
  4.6 1.3 %collective-permute-start.1 = (bf16[128,1024]{1,0:T(8,128)(2,1)S(1)}, bf16[128,1024]{1,0:T(8,128)(2,1)S(1)}, u32[]{:S(2)}, u32[]{:S(2)}) collective-permute-start(bf16[128,1024]{1,0:T(8,128)(2,1)S(1)} %multiply_convert_fusion.1.refs_3_.refs_4_), channel_id=1, source_target_pairs={{1,0},{2,1},{3,2},{4,3},{5,4},{6,5},{7,6},{8,7},{9,8},{10,9},{11,1... | collective-permute-start | bytes 786440 | tf_op jit(solution)/shard_map/ppermute | solution.py:300
  5.9 1.0 %multiply_convert_fusion.2.refs_4_.refs_5_ = bf16[128,512]{1,0:T(8,128)(2,1)S(1)} fusion(bf16[128,4096]{1,0:T(8,128)(2,1)} %param.5, bf16[128,4096]{1,0:T(8,128)(2,1)} %param.7), kind=kLoop, calls=%fused_computation.3 | loop fusion | flops 262144 | bytes 393216 | tf_op jit(solution)/shard_map/convert_element_type | solution.py:299
  6.9 1.3 %collective-permute-start.2 = (bf16[128,512]{1,0:T(8,128)(2,1)S(1)}, bf16[128,512]{1,0:T(8,128)(2,1)S(1)}, u32[]{:S(2)}, u32[]{:S(2)}) collective-permute-start(bf16[128,512]{1,0:T(8,128)(2,1)S(1)} %multiply_convert_fusion.2.refs_4_.refs_5_), channel_id=1, source_target_pairs={{1,0},{2,1},{3,2},{4,3},{5,4},{6,5},{7,6},{8,7},{9,8},{10,9},{11,1... | collective-permute-start | bytes 393224 | tf_op jit(solution)/shard_map/ppermute | solution.py:300
  8.2 0.0 copy-done
  8.3 0.0 copy-done.2
  8.3 3.7 %own_part.1 = (f32[256,128]{1,0:T(8,128)S(1)}, bf16[128,4096]{1,0:T(8,128)(2,1)S(1)}, bf16[2,128,256]{2,1,0:T(8,128)(2,1)S(1)}, bf16[4,32,512]{2,1,0:T(8,128)(2,1)S(1)}) custom-call(s32[1,16]{1,0:T(1,128)S(1)} %copy-done.2, s32[1]{0:T(128)} %bitcast.refs_1_, bf16[128,2560]{1,0:T(8,128)(2,1)S(1)} %multiply_convert_fusion.refs_2_.refs_3_, ...), custom_call_target="tpu_custom_call" | custom-call | flops 2147483648 | bytes 4194304 | tf_op jit(solution)/shard_map/own_part/pallas_call | solution.py:171
  11.9 0.0 collective-permute-done.refs_6_.refs_1_
  11.9 1.7 %lag_part.3.refs_4_ = f32[160,128]{1,0:T(8,128)S(1)} custom-call(bf16[2,128,256]{2,1,0:T(8,128)(2,1)S(1)} %get-tuple-element.12.refs_0_, bf16[128,2560]{1,0:T(8,128)(2,1)S(1)} %collective-permute-done.refs_6_.refs_1_, bf16[128,4096]{1,0:T(8,128)(2,1)S(1)} %get-tuple-element.14.refs_2_, f32[256,128]{1,0:T(8,128)S(1)} %get-tuple-element.15.refs_3_), custom_call_target="tpu_custom_call" | custom-call | flops 1342177280 | bytes 2097152 | tf_op jit(solution)/shard_map/lag_part/pallas_call | solution.py:223
  13.7 0.0 collective-permute-done.1.refs_7_.refs_1_
  13.7 0.9 %lag_part.4.refs_4_ = f32[224,128]{1,0:T(8,128)S(1)} custom-call(bf16[2,128,256]{2,1,0:T(8,128)(2,1)S(1)} %get-tuple-element.12.refs_0_, bf16[128,1024]{1,0:T(8,128)(2,1)S(1)} %collective-permute-done.1.refs_7_.refs_1_, bf16[128,4096]{1,0:T(8,128)(2,1)S(1)} %get-tuple-element.14.refs_2_, f32[256,128]{1,0:T(8,128)S(1)} %get-tuple-element.15.refs_3_, ...), custom_call_target="tpu_custom_call" | custom-call | flops 536870912 | bytes 2097152 | tf_op jit(solution)/shard_map/lag_part/pallas_call | solution.py:223
  14.6 0.0 copy-start.1
  14.6 0.0 collective-permute-done.2.refs_8_.refs_1_
  14.6 1.3 %lag_part.5 = bf16[2,256,128]{2,1,0:T(8,128)(2,1)} custom-call(bf16[2,128,256]{2,1,0:T(8,128)(2,1)S(1)} %get-tuple-element.12.refs_0_, bf16[128,512]{1,0:T(8,128)(2,1)S(1)} %collective-permute-done.2.refs_8_.refs_1_, bf16[128,4096]{1,0:T(8,128)(2,1)S(1)} %get-tuple-element.14.refs_2_, f32[256,128]{1,0:T(8,128)S(1)} %get-tuple-element.15.refs_3_, ...), custom_call_target="tpu_custom_call" | custom-call | flops 268435456 | bytes 2097152 | tf_op jit(solution)/shard_map/lag_part/pallas_call | solution.py:223
  15.9 10.6 %all-to-all-start = ((bf16[32,16,128]{2,1,0:T(8,128)(2,1)}), bf16[32,16,128]{2,1,0:T(8,128)(2,1)S(1)}, u32[]{:S(2)}, u32[]{:S(2)}) async-start(bf16[32,16,128]{2,1,0:T(8,128)(2,1)} %bitcast.1), calls=%async_computation | async-start | bytes 262144 | tf_op jit(solution)/shard_map/all_to_all | solution.py:308
  26.5 0.0 copy-done.1
  26.5 5.4 %down_part.1 = bf16[128,4096]{1,0:T(8,128)(2,1)} custom-call(bf16[2,128,256]{2,1,0:T(8,128)(2,1)S(1)} %get-tuple-element.12.refs_0_, bf16[4,32,512]{2,1,0:T(8,128)(2,1)S(1)} %get-tuple-element.13.refs_1_, f32[256,128]{1,0:T(8,128)S(1)} %copy-done.1, bf16[128,2560]{1,0:T(8,128)(2,1)S(1)} %multiply_convert_fusion.refs_2_.refs_3_, ...), custom_call_target="tpu_custom_call" | custom-call | flops 4294967296 | bytes 4194304 | tf_op jit(solution)/shard_map/down_part/pallas_call | solution.py:270
  31.9 2.8 %all-to-all-done = bf16[32,16,128]{2,1,0:T(8,128)(2,1)S(1)} async-done(((bf16[32,16,128]{2,1,0:T(8,128)(2,1)}), bf16[32,16,128]{2,1,0:T(8,128)(2,1)S(1)}, u32[]{:S(2)}, u32[]{:S(2)}) %all-to-all-start) | async-done | bytes 131104 | tf_op jit(solution)/shard_map/all_to_all | solution.py:308
  34.7 0.6 %convert_reduce_fusion = f32[16,128]{1,0:T(8,128)} fusion(bf16[32,16,128]{2,1,0:T(8,128)(2,1)S(1)} %all-to-all-done), kind=kLoop, calls=%fused_computation.2 | loop fusion | flops 129024 | bytes 139264 | tf_op jit(solution)/shard_map/reduce_sum | solution.py:309
Async XLA Ops:
  2.1 6.2 %copy-start = (bf16[128,4096]{1,0:T(8,128)(2,1)S(1)}, bf16[128,4096]{1,0:T(8,128)(2,1)}, u32[]{:S(2)}) copy-start(bf16[128,4096]{1,0:T(8,128)(2,1)} %refs_5_.1) | copy-start | bytes 3145732
  2.1 6.2 %copy-start.2 = (s32[1,16]{1,0:T(1,128)S(1)}, s32[1,16]{1,0:T(1,128)}, u32[]{:S(2)}) copy-start(s32[1,16]{1,0:T(1,128)} %refs_0_.1) | copy-start | bytes 196
  2.1 9.8 %collective-permute-start = (bf16[128,2560]{1,0:T(8,128)(2,1)S(1)}, bf16[128,2560]{1,0:T(8,128)(2,1)S(1)}, u32[]{:S(2)}, u32[]{:S(2)}) collective-permute-start(bf16[128,2560]{1,0:T(8,128)(2,1)S(1)} %multiply_convert_fusion.refs_2_.refs_3_), channel_id=1, source_target_pairs={{1,0},{2,1},{3,2},{4,3},{5,4},{6,5},{7,6},{8,7},{9,8},{10,9},{11,1... | collective-permute-start | bytes 1966088 | tf_op jit(solution)/shard_map/ppermute | solution.py:300
  4.6 9.0 %collective-permute-start.1 = (bf16[128,1024]{1,0:T(8,128)(2,1)S(1)}, bf16[128,1024]{1,0:T(8,128)(2,1)S(1)}, u32[]{:S(2)}, u32[]{:S(2)}) collective-permute-start(bf16[128,1024]{1,0:T(8,128)(2,1)S(1)} %multiply_convert_fusion.1.refs_3_.refs_4_), channel_id=1, source_target_pairs={{1,0},{2,1},{3,2},{4,3},{5,4},{6,5},{7,6},{8,7},{9,8},{10,9},{11,1... | collective-permute-start | bytes 786440 | tf_op jit(solution)/shard_map/ppermute | solution.py:300
  6.9 7.7 %collective-permute-start.2 = (bf16[128,512]{1,0:T(8,128)(2,1)S(1)}, bf16[128,512]{1,0:T(8,128)(2,1)S(1)}, u32[]{:S(2)}, u32[]{:S(2)}) collective-permute-start(bf16[128,512]{1,0:T(8,128)(2,1)S(1)} %multiply_convert_fusion.2.refs_4_.refs_5_), channel_id=1, source_target_pairs={{1,0},{2,1},{3,2},{4,3},{5,4},{6,5},{7,6},{8,7},{9,8},{10,9},{11,1... | collective-permute-start | bytes 393224 | tf_op jit(solution)/shard_map/ppermute | solution.py:300
  14.6 11.9 %copy-start.1 = (f32[256,128]{1,0:T(8,128)S(1)}, f32[256,128]{1,0:T(8,128)}, u32[]{:S(2)}) copy-start(f32[256,128]{1,0:T(8,128)} %refs_2_.1) | copy-start | bytes 393220
  15.9 18.8 %all-to-all-start = ((bf16[32,16,128]{2,1,0:T(8,128)(2,1)}), bf16[32,16,128]{2,1,0:T(8,128)(2,1)S(1)}, u32[]{:S(2)}, u32[]{:S(2)}) async-start(bf16[32,16,128]{2,1,0:T(8,128)(2,1)} %bitcast.1), calls=%async_computation | async-start | bytes 262144 | tf_op jit(solution)/shard_map/all_to_all | solution.py:308

commit v5 on v4

--- a/solution.py
+++ b/solution.py
@@ -289,7 +289,7 @@
     dp_count = lax.axis_size("dp")
     grad_scale = (1.0 * GROUP * dp_count * local_rows * ctx_count) ** (-0.5)
     place = lax.axis_index("ctx").astype(jnp.int32).reshape(1)
-    cuts = [0, channels * 5 // 8, channels * 7 // 8, channels]
+    cuts = [0, channels * 3 // 4, channels * 7 // 8, channels]
     back = [(i, i - 1) for i in range(1, ctx_count)]
     mixed, halos = [], []
     gate, grad = gate_branch, grad_output

time: 35.7 us -> 35.5 us (level)
  other arithmetic: 4.18 us -> 3.44 us
  starting transfers between devices: 14.6 us -> 15.2 us
    convert_element_type x3 -> x2, other arithmetic: 3.55 us -> 2.81 us  [shards(): (grad[:, low:high].astype(F32) * gate[:, low:high].astype(F32)).astype(BF16)]
    all_to_all x1, starting transfers between devices: 10.6 us -> 11.3 us  [shards(): shared = lax.all_to_all(partial, ('dp', 'ctx'), 0, 0, tiled=True)]
  transfers between devices with their start and end apart: 4 -> 4, of which waited for: 1 -> 1; matrix products, arithmetic and copies ran while one was open for 6% -> 3% of each run, Pallas kernels for 33% -> 33%
where the time goes in v5:
time: 35.5 us; the launch traced here: 35.2 us
  starting transfers between devices  15.2 us (43%)
  Pallas kernels  12.9 us (36%)
  other arithmetic  3.44 us (10%)
  waiting for transfers between devices  2.84 us (8%)
  between operations  0.78 us (2%)
    all_to_all x1, starting transfers between devices, shards(): shared = lax.all_to_all(partial, ('dp', 'ctx'), 0, 0, tiled=True)  11.3 us
    pallas_call x1, Pallas kernels, down_part(): pl.pallas_call(functools.partial(down_kernel, pieces), in_specs=[VMEM] *...  5.37 us
    pallas_call x3, Pallas kernels, lag_part(): pl.pallas_call(functools.partial(lag_kernel, first_group, scale, copies),...  3.91 us
    ppermute x3, starting transfers between devices, shards(): halos.append(lax.ppermute(mixed[-1], 'ctx', back))  3.88 us
    pallas_call x1, Pallas kernels, own_part(): pl.pallas_call(functools.partial(own_kernel, pieces), in_specs=[SMEM, SME...  3.65 us
    all_to_all x1, waiting for transfers between devices, shards(): shared = lax.all_to_all(partial, ('dp', 'ctx'), 0, 0, tiled=True)  2.84 us
    convert_element_type x2, other arithmetic, shards(): (grad[:, low:high].astype(F32) * gate[:, low:high].astype(F32)).astype(BF16)  2.81 us
  transfers between devices with their start and end apart: 4, of which 1 were waited for; matrix products, arithmetic and copies ran while one was open for 3% of the time, Pallas kernels for 33%

profile of v5, /device:TPU:0, one launch (start us, length us, event | category | flops | bytes accessed | tf_op | source)
XLA Modules:
  0.0 35.2 jit_solution(4688600031075293581)
XLA Ops:
  0.6 0.0 copy-start
  0.6 0.0 copy-start.2
  0.6 1.6 %multiply_convert_fusion.refs_2_.refs_3_ = bf16[128,3072]{1,0:T(8,128)(2,1)S(1)} fusion(bf16[128,4096]{1,0:T(8,128)(2,1)} %param.5, bf16[128,4096]{1,0:T(8,128)(2,1)} %param.7), kind=kLoop, calls=%fused_computation | loop fusion | flops 1572864 | bytes 2359296 | tf_op jit(solution)/shard_map/convert_element_type | solution.py:299
  2.3 1.3 %collective-permute-start = (bf16[128,3072]{1,0:T(8,128)(2,1)S(1)}, bf16[128,3072]{1,0:T(8,128)(2,1)S(1)}, u32[]{:S(2)}, u32[]{:S(2)}) collective-permute-start(bf16[128,3072]{1,0:T(8,128)(2,1)S(1)} %multiply_convert_fusion.refs_2_.refs_3_), channel_id=1, source_target_pairs={{1,0},{2,1},{3,2},{4,3},{5,4},{6,5},{7,6},{8,7},{9,8},{10,9},{11,1... | collective-permute-start | bytes 2359304 | tf_op jit(solution)/shard_map/ppermute | solution.py:300
  3.6 1.2 %multiply_convert_fusion.1 = (bf16[128,512]{1,0:T(8,128)(2,1)S(1)}, bf16[128,512]{1,0:T(8,128)(2,1)S(1)}) fusion(bf16[128,4096]{1,0:T(8,128)(2,1)} %param.5, bf16[128,4096]{1,0:T(8,128)(2,1)} %param.7), kind=kLoop, calls=%fused_computation.2 | loop fusion | flops 524288 | bytes 786432 | tf_op jit(solution)/shard_map/convert_element_type | solution.py:299
  4.8 1.3 %collective-permute-start.1 = (bf16[128,512]{1,0:T(8,128)(2,1)S(1)}, bf16[128,512]{1,0:T(8,128)(2,1)S(1)}, u32[]{:S(2)}, u32[]{:S(2)}) collective-permute-start(bf16[128,512]{1,0:T(8,128)(2,1)S(1)} %get-tuple-element.17.refs_3_.refs_4_), channel_id=1, source_target_pairs={{1,0},{2,1},{3,2},{4,3},{5,4},{6,5},{7,6},{8,7},{9,8},{10,9},{11,1... | collective-permute-start | bytes 393224 | tf_op jit(solution)/shard_map/ppermute | solution.py:300
  6.1 1.3 %collective-permute-start.2 = (bf16[128,512]{1,0:T(8,128)(2,1)S(1)}, bf16[128,512]{1,0:T(8,128)(2,1)S(1)}, u32[]{:S(2)}, u32[]{:S(2)}) collective-permute-start(bf16[128,512]{1,0:T(8,128)(2,1)S(1)} %get-tuple-element.16.refs_4_.refs_5_), channel_id=1, source_target_pairs={{1,0},{2,1},{3,2},{4,3},{5,4},{6,5},{7,6},{8,7},{9,8},{10,9},{11,1... | collective-permute-start | bytes 393224 | tf_op jit(solution)/shard_map/ppermute | solution.py:300
  7.4 0.0 copy-done
  7.4 0.0 copy-done.2
  7.4 3.7 %own_part.1 = (f32[256,128]{1,0:T(8,128)S(1)}, bf16[128,4096]{1,0:T(8,128)(2,1)S(1)}, bf16[2,128,256]{2,1,0:T(8,128)(2,1)S(1)}, bf16[4,32,512]{2,1,0:T(8,128)(2,1)S(1)}) custom-call(s32[1,16]{1,0:T(1,128)S(1)} %copy-done.2, s32[1]{0:T(128)} %bitcast.refs_1_, bf16[128,3072]{1,0:T(8,128)(2,1)S(1)} %multiply_convert_fusion.refs_2_.refs_3_, ...), custom_call_target="tpu_custom_call" | custom-call | flops 2147483648 | bytes 4194304 | tf_op jit(solution)/shard_map/own_part/pallas_call | solution.py:171
  11.1 0.0 collective-permute-done.refs_6_.refs_1_
  11.1 2.0 %lag_part.3.refs_4_ = f32[192,128]{1,0:T(8,128)S(1)} custom-call(bf16[2,128,256]{2,1,0:T(8,128)(2,1)S(1)} %get-tuple-element.12.refs_0_, bf16[128,3072]{1,0:T(8,128)(2,1)S(1)} %collective-permute-done.refs_6_.refs_1_, bf16[128,4096]{1,0:T(8,128)(2,1)S(1)} %get-tuple-element.14.refs_2_, f32[256,128]{1,0:T(8,128)S(1)} %get-tuple-element.15.refs_3_), custom_call_target="tpu_custom_call" | custom-call | flops 1610612736 | bytes 2097152 | tf_op jit(solution)/shard_map/lag_part/pallas_call | solution.py:223
  13.1 0.0 collective-permute-done.1.refs_7_.refs_1_
  13.1 0.6 %lag_part.4.refs_4_ = f32[224,128]{1,0:T(8,128)S(1)} custom-call(bf16[2,128,256]{2,1,0:T(8,128)(2,1)S(1)} %get-tuple-element.12.refs_0_, bf16[128,512]{1,0:T(8,128)(2,1)S(1)} %collective-permute-done.1.refs_7_.refs_1_, bf16[128,4096]{1,0:T(8,128)(2,1)S(1)} %get-tuple-element.14.refs_2_, f32[256,128]{1,0:T(8,128)S(1)} %get-tuple-element.15.refs_3_, ...), custom_call_target="tpu_custom_call" | custom-call | flops 268435456 | bytes 2097152 | tf_op jit(solution)/shard_map/lag_part/pallas_call | solution.py:223
  13.7 0.0 copy-start.1
  13.7 0.0 collective-permute-done.2.refs_8_.refs_1_
  13.8 1.3 %lag_part.5 = bf16[2,256,128]{2,1,0:T(8,128)(2,1)} custom-call(bf16[2,128,256]{2,1,0:T(8,128)(2,1)S(1)} %get-tuple-element.12.refs_0_, bf16[128,512]{1,0:T(8,128)(2,1)S(1)} %collective-permute-done.2.refs_8_.refs_1_, bf16[128,4096]{1,0:T(8,128)(2,1)S(1)} %get-tuple-element.14.refs_2_, f32[256,128]{1,0:T(8,128)S(1)} %get-tuple-element.15.refs_3_, ...), custom_call_target="tpu_custom_call" | custom-call | flops 268435456 | bytes 2097152 | tf_op jit(solution)/shard_map/lag_part/pallas_call | solution.py:223
  15.0 11.3 %all-to-all-start = ((bf16[32,16,128]{2,1,0:T(8,128)(2,1)}), bf16[32,16,128]{2,1,0:T(8,128)(2,1)S(1)}, u32[]{:S(2)}, u32[]{:S(2)}) async-start(bf16[32,16,128]{2,1,0:T(8,128)(2,1)} %bitcast.1), calls=%async_computation | async-start | bytes 262144 | tf_op jit(solution)/shard_map/all_to_all | solution.py:308
  26.3 0.0 copy-done.1
  26.3 5.4 %down_part.1 = bf16[128,4096]{1,0:T(8,128)(2,1)} custom-call(bf16[2,128,256]{2,1,0:T(8,128)(2,1)S(1)} %get-tuple-element.12.refs_0_, bf16[4,32,512]{2,1,0:T(8,128)(2,1)S(1)} %get-tuple-element.13.refs_1_, f32[256,128]{1,0:T(8,128)S(1)} %copy-done.1, bf16[128,3072]{1,0:T(8,128)(2,1)S(1)} %multiply_convert_fusion.refs_2_.refs_3_, ...), custom_call_target="tpu_custom_call" | custom-call | flops 4294967296 | bytes 4194304 | tf_op jit(solution)/shard_map/down_part/pallas_call | solution.py:270
  31.7 2.8 %all-to-all-done = bf16[32,16,128]{2,1,0:T(8,128)(2,1)S(1)} async-done(((bf16[32,16,128]{2,1,0:T(8,128)(2,1)}), bf16[32,16,128]{2,1,0:T(8,128)(2,1)S(1)}, u32[]{:S(2)}, u32[]{:S(2)}) %all-to-all-start) | async-done | bytes 131104 | tf_op jit(solution)/shard_map/all_to_all | solution.py:308
  34.6 0.6 %convert_reduce_fusion = f32[16,128]{1,0:T(8,128)} fusion(bf16[32,16,128]{2,1,0:T(8,128)(2,1)S(1)} %all-to-all-done), kind=kLoop, calls=%fused_computation.1 | loop fusion | flops 129024 | bytes 139264 | tf_op jit(solution)/shard_map/reduce_sum | solution.py:309
Async XLA Ops:
  0.6 6.7 %copy-start = (bf16[128,4096]{1,0:T(8,128)(2,1)S(1)}, bf16[128,4096]{1,0:T(8,128)(2,1)}, u32[]{:S(2)}) copy-start(bf16[128,4096]{1,0:T(8,128)(2,1)} %refs_5_.1) | copy-start | bytes 3145732
  0.6 6.7 %copy-start.2 = (s32[1,16]{1,0:T(1,128)S(1)}, s32[1,16]{1,0:T(1,128)}, u32[]{:S(2)}) copy-start(s32[1,16]{1,0:T(1,128)} %refs_0_.1) | copy-start | bytes 196
  2.3 8.8 %collective-permute-start = (bf16[128,3072]{1,0:T(8,128)(2,1)S(1)}, bf16[128,3072]{1,0:T(8,128)(2,1)S(1)}, u32[]{:S(2)}, u32[]{:S(2)}) collective-permute-start(bf16[128,3072]{1,0:T(8,128)(2,1)S(1)} %multiply_convert_fusion.refs_2_.refs_3_), channel_id=1, source_target_pairs={{1,0},{2,1},{3,2},{4,3},{5,4},{6,5},{7,6},{8,7},{9,8},{10,9},{11,1... | collective-permute-start | bytes 2359304 | tf_op jit(solution)/shard_map/ppermute | solution.py:300
  4.8 8.3 %collective-permute-start.1 = (bf16[128,512]{1,0:T(8,128)(2,1)S(1)}, bf16[128,512]{1,0:T(8,128)(2,1)S(1)}, u32[]{:S(2)}, u32[]{:S(2)}) collective-permute-start(bf16[128,512]{1,0:T(8,128)(2,1)S(1)} %get-tuple-element.17.refs_3_.refs_4_), channel_id=1, source_target_pairs={{1,0},{2,1},{3,2},{4,3},{5,4},{6,5},{7,6},{8,7},{9,8},{10,9},{11,1... | collective-permute-start | bytes 393224 | tf_op jit(solution)/shard_map/ppermute | solution.py:300
  6.1 7.7 %collective-permute-start.2 = (bf16[128,512]{1,0:T(8,128)(2,1)S(1)}, bf16[128,512]{1,0:T(8,128)(2,1)S(1)}, u32[]{:S(2)}, u32[]{:S(2)}) collective-permute-start(bf16[128,512]{1,0:T(8,128)(2,1)S(1)} %get-tuple-element.16.refs_4_.refs_5_), channel_id=1, source_target_pairs={{1,0},{2,1},{3,2},{4,3},{5,4},{6,5},{7,6},{8,7},{9,8},{10,9},{11,1... | collective-permute-start | bytes 393224 | tf_op jit(solution)/shard_map/ppermute | solution.py:300
  13.7 12.6 %copy-start.1 = (f32[256,128]{1,0:T(8,128)S(1)}, f32[256,128]{1,0:T(8,128)}, u32[]{:S(2)}) copy-start(f32[256,128]{1,0:T(8,128)} %refs_2_.1) | copy-start | bytes 393220
  15.0 19.5 %all-to-all-start = ((bf16[32,16,128]{2,1,0:T(8,128)(2,1)}), bf16[32,16,128]{2,1,0:T(8,128)(2,1)S(1)}, u32[]{:S(2)}, u32[]{:S(2)}) async-start(bf16[32,16,128]{2,1,0:T(8,128)(2,1)} %bitcast.1), calls=%async_computation | async-start | bytes 262144 | tf_op jit(solution)/shard_map/all_to_all | solution.py:308

commit v6 on v5

--- a/solution.py
+++ b/solution.py
@@ -163,6 +163,7 @@
             product = correlate(x_back, step, stacked).reshape(PAIRS, BLOCK, TILE) * back_ref[step][None]
             total = product if total is None else total + product
         lag_ref[groups] = lag_sums(total.reshape(PAIRS * BLOCK, TILE))
+        xb_ref[:, at * TILE : (at + 1) * TILE] = x_back * keep_ref[0]
 
 
 def own_part(lens, place, mixed, x):
@@ -201,7 +202,7 @@
     for t in range(halo_ref.shape[1] // TILE):
         low, high = halves(halo_ref[:, t * TILE : (t + 1) * TILE] * keep_ref[1])
         at = first_group * GROUP + t * TILE
-        x_back = xb_ref[:, at : at + TILE] * keep_ref[0]
+        x_back = xb_ref[:, at : at + TILE]
         total = None
         for step in range(STEPS):
             stacked = jnp.concatenate([turned_cross(low, step), turned_cross(high, step)], axis=0)
@@ -289,7 +290,7 @@
     dp_count = lax.axis_size("dp")
     grad_scale = (1.0 * GROUP * dp_count * local_rows * ctx_count) ** (-0.5)
     place = lax.axis_index("ctx").astype(jnp.int32).reshape(1)
-    cuts = [0, channels * 3 // 4, channels * 7 // 8, channels]
+    cuts = [0, channels * 5 // 8, channels * 13 // 16, channels]
     back = [(i, i - 1) for i in range(1, ctx_count)]
     mixed, halos = [], []
     gate, grad = gate_branch, grad_output

time: 35.5 us -> 35.5 us (level)
  transfers between devices with their start and end apart: 4 -> 4, of which waited for: 1 -> 1; matrix products, arithmetic and copies ran while one was open for 3% -> 4% of each run, Pallas kernels for 33% -> 33%
where the time goes in v6:
time: 35.5 us; the launch traced here: 35.2 us
  starting transfers between devices  15.3 us (43%)
  Pallas kernels  12.8 us (36%)
  other arithmetic  3.39 us (10%)
  waiting for transfers between devices  2.84 us (8%)
  between operations  0.77 us (2%)
    all_to_all x1, starting transfers between devices, shards(): shared = lax.all_to_all(partial, ('dp', 'ctx'), 0, 0, tiled=True)  11.3 us
    pallas_call x1, Pallas kernels, down_part(): pl.pallas_call(functools.partial(down_kernel, pieces), in_specs=[VMEM] *...  5.37 us
    ppermute x3, starting transfers between devices, shards(): halos.append(lax.ppermute(mixed[-1], 'ctx', back))  4.01 us
    pallas_call x3, Pallas kernels, lag_part(): pl.pallas_call(functools.partial(lag_kernel, first_group, scale, copies),...  3.76 us
    pallas_call x1, Pallas kernels, own_part(): pl.pallas_call(functools.partial(own_kernel, pieces), in_specs=[SMEM, SME...  3.7 us
    all_to_all x1, waiting for transfers between devices, shards(): shared = lax.all_to_all(partial, ('dp', 'ctx'), 0, 0, tiled=True)  2.84 us
    convert_element_type x2, other arithmetic, shards(): (grad[:, low:high].astype(F32) * gate[:, low:high].astype(F32)).astype(BF16)  2.76 us
  transfers between devices with their start and end apart: 4, of which 1 were waited for; matrix products, arithmetic and copies ran while one was open for 4% of the time, Pallas kernels for 33%

profile of v6, /device:TPU:0, one launch (start us, length us, event | category | flops | bytes accessed | tf_op | source)
XLA Modules:
  0.0 35.2 jit_solution(4704708950531963695)
XLA Ops:
  0.6 1.4 %multiply_convert_fusion.refs_2_.refs_3_ = bf16[128,2560]{1,0:T(8,128)(2,1)S(1)} fusion(bf16[128,4096]{1,0:T(8,128)(2,1)} %param.5, bf16[128,4096]{1,0:T(8,128)(2,1)} %param.7), kind=kLoop, calls=%fused_computation | loop fusion | flops 1310720 | bytes 1966080 | tf_op jit(solution)/shard_map/convert_element_type | solution.py:300
  2.1 0.0 copy-start
  2.1 0.0 copy-start.2
  2.1 1.4 %collective-permute-start = (bf16[128,2560]{1,0:T(8,128)(2,1)S(1)}, bf16[128,2560]{1,0:T(8,128)(2,1)S(1)}, u32[]{:S(2)}, u32[]{:S(2)}) collective-permute-start(bf16[128,2560]{1,0:T(8,128)(2,1)S(1)} %multiply_convert_fusion.refs_2_.refs_3_), channel_id=1, source_target_pairs={{1,0},{2,1},{3,2},{4,3},{5,4},{6,5},{7,6},{8,7},{9,8},{10,9},{11,1... | collective-permute-start | bytes 1966088 | tf_op jit(solution)/shard_map/ppermute | solution.py:301
  3.5 1.3 %multiply_convert_fusion.1 = (bf16[128,768]{1,0:T(8,128)(2,1)S(1)}, bf16[128,768]{1,0:T(8,128)(2,1)S(1)}) fusion(bf16[128,4096]{1,0:T(8,128)(2,1)} %param.5, bf16[128,4096]{1,0:T(8,128)(2,1)} %param.7), kind=kLoop, calls=%fused_computation.1 | loop fusion | flops 786432 | bytes 1179648 | tf_op jit(solution)/shard_map/convert_element_type | solution.py:300
  4.8 1.3 %collective-permute-start.1 = (bf16[128,768]{1,0:T(8,128)(2,1)S(1)}, bf16[128,768]{1,0:T(8,128)(2,1)S(1)}, u32[]{:S(2)}, u32[]{:S(2)}) collective-permute-start(bf16[128,768]{1,0:T(8,128)(2,1)S(1)} %get-tuple-element.17.refs_3_.refs_4_), channel_id=1, source_target_pairs={{1,0},{2,1},{3,2},{4,3},{5,4},{6,5},{7,6},{8,7},{9,8},{10,9},{11,1... | collective-permute-start | bytes 589832 | tf_op jit(solution)/shard_map/ppermute | solution.py:301
  6.1 1.3 %collective-permute-start.2 = (bf16[128,768]{1,0:T(8,128)(2,1)S(1)}, bf16[128,768]{1,0:T(8,128)(2,1)S(1)}, u32[]{:S(2)}, u32[]{:S(2)}) collective-permute-start(bf16[128,768]{1,0:T(8,128)(2,1)S(1)} %get-tuple-element.16.refs_4_.refs_5_), channel_id=1, source_target_pairs={{1,0},{2,1},{3,2},{4,3},{5,4},{6,5},{7,6},{8,7},{9,8},{10,9},{11,1... | collective-permute-start | bytes 589832 | tf_op jit(solution)/shard_map/ppermute | solution.py:301
  7.5 0.0 copy-done
  7.5 0.0 copy-done.2
  7.5 3.7 %own_part.1 = (f32[256,128]{1,0:T(8,128)S(1)}, bf16[128,4096]{1,0:T(8,128)(2,1)S(1)}, bf16[2,128,256]{2,1,0:T(8,128)(2,1)S(1)}, bf16[4,32,512]{2,1,0:T(8,128)(2,1)S(1)}) custom-call(s32[1,16]{1,0:T(1,128)S(1)} %copy-done.2, s32[1]{0:T(128)} %bitcast.refs_1_, bf16[128,2560]{1,0:T(8,128)(2,1)S(1)} %multiply_convert_fusion.refs_2_.refs_3_, ...), custom_call_target="tpu_custom_call" | custom-call | flops 2147483648 | bytes 4194304 | tf_op jit(solution)/shard_map/own_part/pallas_call | solution.py:172
  11.2 0.0 collective-permute-done.refs_6_.refs_1_
  11.2 1.7 %lag_part.3.refs_4_ = f32[160,128]{1,0:T(8,128)S(1)} custom-call(bf16[2,128,256]{2,1,0:T(8,128)(2,1)S(1)} %get-tuple-element.12.refs_0_, bf16[128,2560]{1,0:T(8,128)(2,1)S(1)} %collective-permute-done.refs_6_.refs_1_, bf16[128,4096]{1,0:T(8,128)(2,1)S(1)} %get-tuple-element.14.refs_2_, f32[256,128]{1,0:T(8,128)S(1)} %get-tuple-element.15.refs_3_), custom_call_target="tpu_custom_call" | custom-call | flops 1342177280 | bytes 2097152 | tf_op jit(solution)/shard_map/lag_part/pallas_call | solution.py:224
  12.9 0.0 collective-permute-done.1.refs_7_.refs_1_
  12.9 0.7 %lag_part.4.refs_4_ = f32[208,128]{1,0:T(8,128)S(1)} custom-call(bf16[2,128,256]{2,1,0:T(8,128)(2,1)S(1)} %get-tuple-element.12.refs_0_, bf16[128,768]{1,0:T(8,128)(2,1)S(1)} %collective-permute-done.1.refs_7_.refs_1_, bf16[128,4096]{1,0:T(8,128)(2,1)S(1)} %get-tuple-element.14.refs_2_, f32[256,128]{1,0:T(8,128)S(1)} %get-tuple-element.15.refs_3_, ...), custom_call_target="tpu_custom_call" | custom-call | flops 402653184 | bytes 2097152 | tf_op jit(solution)/shard_map/lag_part/pallas_call | solution.py:224
  13.6 0.0 copy-start.1
  13.6 0.0 collective-permute-done.2.refs_8_.refs_1_
  13.7 1.3 %lag_part.5 = bf16[2,256,128]{2,1,0:T(8,128)(2,1)} custom-call(bf16[2,128,256]{2,1,0:T(8,128)(2,1)S(1)} %get-tuple-element.12.refs_0_, bf16[128,768]{1,0:T(8,128)(2,1)S(1)} %collective-permute-done.2.refs_8_.refs_1_, bf16[128,4096]{1,0:T(8,128)(2,1)S(1)} %get-tuple-element.14.refs_2_, f32[256,128]{1,0:T(8,128)S(1)} %get-tuple-element.15.refs_3_, ...), custom_call_target="tpu_custom_call" | custom-call | flops 402653184 | bytes 2097152 | tf_op jit(solution)/shard_map/lag_part/pallas_call | solution.py:224
  15.0 11.3 %all-to-all-start = ((bf16[32,16,128]{2,1,0:T(8,128)(2,1)}), bf16[32,16,128]{2,1,0:T(8,128)(2,1)S(1)}, u32[]{:S(2)}, u32[]{:S(2)}) async-start(bf16[32,16,128]{2,1,0:T(8,128)(2,1)} %bitcast.1), calls=%async_computation | async-start | bytes 262144 | tf_op jit(solution)/shard_map/all_to_all | solution.py:309
  26.3 0.0 copy-done.1
  26.3 5.4 %down_part.1 = bf16[128,4096]{1,0:T(8,128)(2,1)} custom-call(bf16[2,128,256]{2,1,0:T(8,128)(2,1)S(1)} %get-tuple-element.12.refs_0_, bf16[4,32,512]{2,1,0:T(8,128)(2,1)S(1)} %get-tuple-element.13.refs_1_, f32[256,128]{1,0:T(8,128)S(1)} %copy-done.1, bf16[128,2560]{1,0:T(8,128)(2,1)S(1)} %multiply_convert_fusion.refs_2_.refs_3_, ...), custom_call_target="tpu_custom_call" | custom-call | flops 4294967296 | bytes 4194304 | tf_op jit(solution)/shard_map/down_part/pallas_call | solution.py:271
  31.7 2.8 %all-to-all-done = bf16[32,16,128]{2,1,0:T(8,128)(2,1)S(1)} async-done(((bf16[32,16,128]{2,1,0:T(8,128)(2,1)}), bf16[32,16,128]{2,1,0:T(8,128)(2,1)S(1)}, u32[]{:S(2)}, u32[]{:S(2)}) %all-to-all-start) | async-done | bytes 131104 | tf_op jit(solution)/shard_map/all_to_all | solution.py:309
  34.5 0.6 %convert_reduce_fusion = f32[16,128]{1,0:T(8,128)} fusion(bf16[32,16,128]{2,1,0:T(8,128)(2,1)S(1)} %all-to-all-done), kind=kLoop, calls=%fused_computation.3 | loop fusion | flops 129024 | bytes 139264 | tf_op jit(solution)/shard_map/reduce_sum | solution.py:310
Async XLA Ops:
  2.1 5.4 %copy-start = (bf16[128,4096]{1,0:T(8,128)(2,1)S(1)}, bf16[128,4096]{1,0:T(8,128)(2,1)}, u32[]{:S(2)}) copy-start(bf16[128,4096]{1,0:T(8,128)(2,1)} %refs_5_.1) | copy-start | bytes 3145732
  2.1 5.4 %copy-start.2 = (s32[1,16]{1,0:T(1,128)S(1)}, s32[1,16]{1,0:T(1,128)}, u32[]{:S(2)}) copy-start(s32[1,16]{1,0:T(1,128)} %refs_0_.1) | copy-start | bytes 196
  2.1 9.1 %collective-permute-start = (bf16[128,2560]{1,0:T(8,128)(2,1)S(1)}, bf16[128,2560]{1,0:T(8,128)(2,1)S(1)}, u32[]{:S(2)}, u32[]{:S(2)}) collective-permute-start(bf16[128,2560]{1,0:T(8,128)(2,1)S(1)} %multiply_convert_fusion.refs_2_.refs_3_), channel_id=1, source_target_pairs={{1,0},{2,1},{3,2},{4,3},{5,4},{6,5},{7,6},{8,7},{9,8},{10,9},{11,1... | collective-permute-start | bytes 1966088 | tf_op jit(solution)/shard_map/ppermute | solution.py:301
  4.8 8.1 %collective-permute-start.1 = (bf16[128,768]{1,0:T(8,128)(2,1)S(1)}, bf16[128,768]{1,0:T(8,128)(2,1)S(1)}, u32[]{:S(2)}, u32[]{:S(2)}) collective-permute-start(bf16[128,768]{1,0:T(8,128)(2,1)S(1)} %get-tuple-element.17.refs_3_.refs_4_), channel_id=1, source_target_pairs={{1,0},{2,1},{3,2},{4,3},{5,4},{6,5},{7,6},{8,7},{9,8},{10,9},{11,1... | collective-permute-start | bytes 589832 | tf_op jit(solution)/shard_map/ppermute | solution.py:301
  6.1 7.5 %collective-permute-start.2 = (bf16[128,768]{1,0:T(8,128)(2,1)S(1)}, bf16[128,768]{1,0:T(8,128)(2,1)S(1)}, u32[]{:S(2)}, u32[]{:S(2)}) collective-permute-start(bf16[128,768]{1,0:T(8,128)(2,1)S(1)} %get-tuple-element.16.refs_4_.refs_5_), channel_id=1, source_target_pairs={{1,0},{2,1},{3,2},{4,3},{5,4},{6,5},{7,6},{8,7},{9,8},{10,9},{11,1... | collective-permute-start | bytes 589832 | tf_op jit(solution)/shard_map/ppermute | solution.py:301
  13.6 12.7 %copy-start.1 = (f32[256,128]{1,0:T(8,128)S(1)}, f32[256,128]{1,0:T(8,128)}, u32[]{:S(2)}) copy-start(f32[256,128]{1,0:T(8,128)} %refs_2_.1) | copy-start | bytes 393220
  15.0 19.5 %all-to-all-start = ((bf16[32,16,128]{2,1,0:T(8,128)(2,1)}), bf16[32,16,128]{2,1,0:T(8,128)(2,1)S(1)}, u32[]{:S(2)}, u32[]{:S(2)}) async-start(bf16[32,16,128]{2,1,0:T(8,128)(2,1)} %bitcast.1), calls=%async_computation | async-start | bytes 262144 | tf_op jit(solution)/shard_map/all_to_all | solution.py:309
